TPU v7x, 128 devices: a whole 4x4x4 slice. The times are simulated.
128 devices in a mesh: dp: 8 (over x, core), expert: 16 (over z, y).
Axes of the slice: x: 4, y: 4, z: 4, core: 2. Of those that a mesh axis runs over, the one named last changes fastest.
Arguments:
- tokens: bfloat16 [32768, 7168], P(('dp', 'expert')), may hold values from -6 to 6
- routes: int32 [32768, 2], P(('dp', 'expert')), may hold values from 0 to 15, all different within a row; in each aligned block of 256 rows (0 to 255, 256 to 511, ...) at most 64 rows name the same one
- weight: bfloat16 [16, 2048, 7168], P('expert', 'dp'), may hold values from -6 to 6
- levels: int32 [16, 2048], P('expert', 'dp'), may hold values from 4 to 16
- pivots: float32 [16, 128], P('expert'), may hold values from 0.5 to 1.5
- panel_diag: float32 [16, 128, 128], P('expert'), may hold values from -1.5 to 1.5
- panel_rest: float32 [16, 128, 7040], P('expert', None, 'dp'), may hold values from -1.5 to 1.5
Outputs:
- hessian: float32 [16, 512, 7168], P('expert', 'dp')
- quantized: float32 [16, 2048, 128], P('expert', 'dp')
- remainder: float32 [16, 2048, 7040], P('expert', 'dp')
Inputs may be any that keep to these rules, and one draw needn't show every extreme that they name: `routes`: the 2 experts of a token differ. Among the rows of one device no expert is named by more than 64 tokens, and some device's rows name some expert exactly 64 times. Every expert is named by some token.
All inputs are finite; a program needn't handle non-finite values.
Results may differ from a plain program's by a relative error of at most 0.00055.
Values may be sent and summed in bfloat16 or wider, within the bound.
No kernel may reach another device: no remote copies, remote signals or barrier semaphores. Data moves between devices by JAX's collectives and lax.ppermute only.
A program may use at most 128 MiB of HBM per device.

v0:
```python
import math

import jax
import jax.numpy as jnp
from jax import lax
from jax.sharding import PartitionSpec as P

HROWS = 512
BLOCK = 128


def smooth_grid(values, spacing):
    return values - 0.9 * spacing / (2.0 * math.pi) * jnp.sin(2.0 * math.pi * values / spacing)


def block_update(block_cols, spacing, strict_upper, pivots):
    width = block_cols.shape[1]

    def advance(column, carry):
        current, snapped_all, errors = carry
        column = jnp.asarray(column).astype(jnp.int32)
        values = lax.dynamic_slice_in_dim(current, column, 1, 1)
        snapped = smooth_grid(values, spacing)
        scaled = (values - snapped) / lax.dynamic_slice_in_dim(pivots, column, 1, 0)[None, :]
        upper_row = lax.dynamic_slice_in_dim(strict_upper, column, 1, 0)
        current = current - scaled * upper_row
        snapped_all = lax.dynamic_update_slice_in_dim(snapped_all, snapped, column, 1)
        errors = lax.dynamic_update_slice_in_dim(errors, scaled, column, 1)
        return (current, snapped_all, errors)

    zeros = jnp.zeros_like(block_cols)
    final_block, snapped_all, errors = lax.fori_loop(0, width, advance, (block_cols, zeros, zeros))
    return (snapped_all, errors)


def on_device(tokens, routes, weight, levels, pivots, panel_diag, panel_rest):
    expert_count = lax.axis_size("expert")
    tok_rows = tokens.shape[0]
    top_count = routes.shape[1]
    capacity = tok_rows * top_count * 2 // expert_count
    width = tokens.shape[1]
    flat_routes = routes.reshape(-1)
    onehot = (flat_routes[:, None] == jnp.arange(expert_count, dtype=jnp.int32)[None, :]).astype(
        jnp.int32
    )
    earlier = jnp.cumsum(onehot, axis=0) - onehot
    within = jnp.sum(earlier * onehot, axis=1)
    target = flat_routes * capacity + within
    source_row = jnp.arange(flat_routes.shape[0], dtype=jnp.int32) // top_count
    slot_source = jnp.zeros((expert_count * capacity,), jnp.int32).at[target].set(source_row)
    slot_filled = jnp.zeros((expert_count * capacity,), jnp.int32).at[target].set(1)
    outgoing = jnp.where(slot_filled[:, None] > 0, tokens[slot_source], jnp.zeros((), tokens.dtype))
    outgoing = outgoing.reshape(expert_count, capacity, width)
    local_counts = jnp.sum(onehot, axis=0).astype(jnp.float32)
    received = lax.all_to_all(outgoing, "expert", split_axis=0, concat_axis=0, tiled=True)
    received = received.reshape(expert_count * capacity, width)
    totals = lax.psum(local_counts, ("dp", "expert"))
    own_count = jnp.sum(
        totals
        * (jnp.arange(expert_count, dtype=jnp.int32) == lax.axis_index("expert")).astype(
            jnp.float32
        )
    )
    share_rows = HROWS // lax.axis_size("dp")
    partial_value = jnp.einsum(
        "tr,tc->rc", received[:, :HROWS], received, preferred_element_type=jnp.float32
    )
    summed = lax.psum(partial_value, "dp")
    share = lax.dynamic_slice_in_dim(summed, lax.axis_index("dp") * share_rows, share_rows, 0)
    hessian = (share * (2.0 / own_count))[None]
    weight_rows = weight[0]
    block_cols = weight_rows[:, :BLOCK].astype(jnp.float32)
    spacing = (jnp.max(jnp.abs(block_cols), axis=1, keepdims=True) + 1e-05) / levels[0].astype(
        jnp.float32
    )[:, None]
    strict_upper = jnp.triu(panel_diag[0], 1)
    snapped_all, errors = block_update(block_cols, spacing, strict_upper, pivots[0])
    piece = lax.all_gather(panel_rest.astype(jnp.bfloat16), "dp", axis=2, tiled=True).astype(
        jnp.float32
    )
    older = lax.dynamic_slice_in_dim(weight_rows, BLOCK, piece.shape[2], 1).astype(jnp.float32)
    remainder = older - jnp.dot(
        errors, piece[0], precision=lax.Precision.HIGHEST, preferred_element_type=jnp.float32
    )
    return (hessian, snapped_all[None], remainder[None])


def solution(mesh):
    return jax.shard_map(
        on_device,
        mesh=mesh,
        in_specs=(
            P(("dp", "expert"), None),
            P(("dp", "expert"), None),
            P("expert", "dp", None),
            P("expert", "dp"),
            P("expert", None),
            P("expert", None, None),
            P("expert", None, "dp"),
        ),
        out_specs=(P("expert", "dp", None), P("expert", "dp", None), P("expert", "dp", None)),
        check_vma=False,
    )
```

profile of v0, /device:TPU:6, one launch (start us, length us, event | category | flops | bytes accessed | tf_op | source)
XLA Modules:
  0.0 575.4 jit_solution(6969189890675146959)
XLA Ops:
  7.2 0.8 copy.11
  9.0 1.2 reduce-window.6
  10.8 2.4 scatter_custom_fusion.1
  13.3 2.4 scatter_custom_fusion
  15.9 27.3 %gather_fusion = bf16[1024,7168]{1,0:T(8,128)(2,1)} fusion(bf16[256,7168]{1,0:T(8,128)(2,1)} %param.9, s32[1024]{0:T(1024)S(1)} %fusion.7), kind=kCustom, calls=%fused_computation | custom fusion | bytes 29364224 | tf_op jit(solution)/shard_map/gather | solution.py:52
  43.1 13.5 %broadcast_select_fusion = bf16[16,64,7168]{2,1,0:T(8,128)(2,1)} fusion(bf16[16,64,7168]{2,1,0:T(8,128)(2,1)} %bitcast.42, pred[16,64]{1,0:T(8,128)(4,1)S(1)} %broadcast_in_dim.46), kind=kLoop, calls=%fused_computation.9 | loop fusion | flops 7340032 | bytes 29361152 | tf_op jit(solution)/shard_map/jit(_where)/select_n | solution.py:52
  56.6 8.2 %all-to-all-start = ((bf16[16,64,7168]{2,1,0:T(8,128)(2,1)}), bf16[16,64,7168]{2,1,0:T(8,128)(2,1)}, u32[]{:S(2)}, u32[]{:S(2)}) async-start(bf16[16,64,7168]{2,1,0:T(8,128)(2,1)} %broadcast_select_fusion), calls=%async_computation | async-start | bytes 29360128 | tf_op jit(solution)/shard_map/all_to_all | solution.py:55
  64.9 0.7 convert_element_type.41
  65.7 0.9 slice_convert_fusion
  66.7 1.0 abs_reduce_fusion
  67.7 215.4 %all-to-all-done = bf16[16,64,7168]{2,1,0:T(8,128)(2,1)} async-done(((bf16[16,64,7168]{2,1,0:T(8,128)(2,1)}), bf16[16,64,7168]{2,1,0:T(8,128)(2,1)}, u32[]{:S(2)}, u32[]{:S(2)}) %all-to-all-start) | async-done | bytes 14680096 | tf_op jit(solution)/shard_map/all_to_all | solution.py:55
  283.1 14.7 %fusion.2 = f32[512,7168]{1,0:T(8,128)} fusion(bf16[1024,7168]{1,0:T(8,128)(2,1)} %bitcast.7), kind=kOutput, calls=%fused_computation.14 | convolution fusion | flops 7516192768 | bytes 30408704 | tf_op jit(solution)/shard_map/tr,tc->rc/dot_general | solution.py:65
  298.4 195.2 %while.19 = (s32[]{:T(128)}, f32[256,128]{0,1:T(8,128)S(1)}, f32[256,128]{0,1:T(8,128)S(1)}, f32[256,128]{0,1:T(8,128)S(1)}, f32[256,1]{0,1:T(1,128)S(1)}, /*ind...) while((s32[]{:T(128)}, f32[256,128]{0,1:T(8,128)S(1)}, f32[256,128]{0,1:T(8,128)S(1)}, ...), condition=%wide.region_11.12_spmd, body=%wide.region_10.11_spmd.sunk | while | flops 67330 | bytes 273021 | solution.py:32
  303.5 0.7 subtract_divide_fusion.2
  305.1 0.7 subtract_divide_fusion.2
  349.3 0.7 subtract_divide_fusion.2
  356.9 0.7 subtract_divide_fusion.2
  367.6 0.7 subtract_divide_fusion.2
  370.7 0.7 subtract_divide_fusion.2
  385.9 0.7 subtract_divide_fusion.2
  387.5 0.7 subtract_divide_fusion.2
  389.0 0.7 subtract_divide_fusion.2
  390.5 0.7 subtract_divide_fusion.2
  396.6 0.7 subtract_divide_fusion.2
  408.8 0.7 subtract_divide_fusion.2
  421.0 0.7 subtract_divide_fusion.2
  433.2 0.7 subtract_divide_fusion.2
  440.9 0.7 subtract_divide_fusion.2
  493.6 62.6 %psum.15 = f32[16]{0:T(128)S(1)} all-reduce(f32[16]{0:T(128)S(1)} %convert_element_type.36), channel_id=1, replica_groups=mesh['dp'=8,'expert'=16] {'dp','expert'}, use_global_device_ids=true, to_apply=%region_7.8 | all-reduce | flops 16 | bytes 128 | tf_op jit(solution)/shard_map/psum | solution.py:57
  556.2 0.8 copy.15
  558.3 7.4 %fusion = f32[1,256,7040]{2,1,0:T(8,128)} fusion(f32[256,128]{0,1:T(8,128)S(1)} %get-tuple-element.181, bf16[256,7168]{1,0:T(8,128)(2,1)} %bitcast.45, bf16[1,128,7040]{1,2,0:T(8,128)(2,1)} %all-gather.2.cloned.1.call-done), kind=kOutput, calls=%fused_computation.11 | convolution fusion | flops 2771845120 | bytes 12746752 | tf_op jit(solution)/shard_map/dot_general | solution.py:82
  565.7 2.9 multiply_bitcast_fusion
  (791 shorter events, 182.1 us)
Async XLA Ops:
  56.6 8.3 %copy-start = (f32[1,128,880]{1,2,0:T(8,128)S(1)}, f32[1,128,880]{1,2,0:T(8,128)}, u32[]{:S(2)}) copy-start(f32[1,128,880]{1,2,0:T(8,128)} %param.15) | copy-start | bytes 1351684
  56.6 11.0 %copy-start.2 = (s32[1,256]{1,0:T(1,128)S(1)}, s32[1,256]{1,0:T(1,128)}, u32[]{:S(2)}) copy-start(s32[1,256]{1,0:T(1,128)} %param.12) | copy-start | bytes 3076
  56.6 11.1 %copy-start.1 = (f32[1,128,128]{2,1,0:T(8,128)S(1)}, f32[1,128,128]{2,1,0:T(8,128)}, u32[]{:S(2)}) copy-start(f32[1,128,128]{2,1,0:T(8,128)} %param.14) | copy-start | bytes 196612
  56.6 226.5 %all-to-all-start = ((bf16[16,64,7168]{2,1,0:T(8,128)(2,1)}), bf16[16,64,7168]{2,1,0:T(8,128)(2,1)}, u32[]{:S(2)}, u32[]{:S(2)}) async-start(bf16[16,64,7168]{2,1,0:T(8,128)(2,1)} %broadcast_select_fusion), calls=%async_computation | async-start | bytes 29360128 | tf_op jit(solution)/shard_map/all_to_all | solution.py:55
  64.8 493.5 %all-gather.2.cloned.1.call-start = ((), (), s32[]{:S(2)}) async-start(), calls=%async_computation.2 | async-start | bytes 2027520 | tf_op jit(solution)/shard_map/all_gather | solution.py:78
  65.6 500.1 %all-reduce.2.cloned.1.call-start = ((), (), s32[]{:S(2)}) async-start(), calls=%async_computation.1 | async-start | bytes 29360128 | tf_op jit(solution)/shard_map/psum | solution.py:68
  297.7 0.7 copy-start.3
Sparse Core Ops, SparseCore 0:
  67.9 24.6 all-gather.1
  297.9 159.9 all-reduce.1
where the time goes:
time: 581 us; the launch traced here: 575 us
  waiting for transfers between devices  215 us (37%)
  other arithmetic  124 us (21%)
  local copies, waits for them, and re-layouts  123 us (21%)
  blocking collectives  62.6 us (11%)
  matrix products  22.1 us (4%)
  between operations  14.9 us (3%)
  starting transfers between devices  8.31 us (1%)
    all_to_all x1, waiting for transfers between devices, on_device(): lax.all_to_all(outgoing, 'expert', split_axis=0, concat_axis=0, tiled=True)  215 us
    div x128, other arithmetic, advance(): (values - snapped) / lax.dynamic_slice_in_dim(pivots, column, 1, 0)[None, :]  90.4 us
    dynamic_slice x128, local copies, waits for them, and re-layouts, advance(): lax.dynamic_slice_in_dim(pivots, column, 1, 0)[None, :]  75 us
    psum x1, blocking collectives, on_device(): totals = lax.psum(local_counts, ('dp', 'expert'))  62.6 us
    gather x1, local copies, waits for them, and re-layouts, on_device(): tokens[slot_source]  27.3 us
    dot_general x1, matrix products, on_device(): jnp.einsum('tr,tc->rc', received[:, :HROWS], received, preferred_element_...  14.7 us
    select_n x1, other arithmetic, on_device(): jnp.where(slot_filled[:, None] > 0, tokens[slot_source], jnp.zeros((), to...  13.5 us
  transfers between devices with their start and end apart: 3, of which 1 were waited for; matrix products, arithmetic and copies ran while one was open for 37% of the time, Pallas kernels for 0%

commit v1 on v0

v1 whole, which is shorter than its diff:
```python
import functools
import math

import jax
import jax.numpy as jnp
import numpy as np
from jax import lax
from jax.experimental import pallas as pl
from jax.experimental.pallas import tpu as pltpu
from jax.sharding import Mesh
from jax.sharding import PartitionSpec as P

BLOCK = 128
PLANE = ("z", "y")
EXPERTS = 16
TOK = 256
CAP = 64
MIB = 1024 * 1024
UP = [(i, (i + 1) % 4) for i in range(4)]
DOWN = [(i, (i - 1) % 4) for i in range(4)]
OPPOSITE = [(i, (i + 2) % 4) for i in range(4)]
SWAP = [(0, 1), (1, 0)]
bf16, f16, f32, i32 = jnp.bfloat16, jnp.float16, jnp.float32, jnp.int32
SLAB_ROWS, ROUTE_ROWS = 4 * TOK, 16
FIRST_ROWS = SLAB_ROWS + ROUTE_ROWS + 2 * TOK
SECOND_ROWS = TOK + TOK // 2
EXTRA = 16


def sine_coefficients():
    nodes = 0.5 * np.cos(np.pi * (np.arange(400) + 0.5) / 800)
    powers = np.stack([nodes ** (2 * k + 1) for k in range(8)], 1)
    scale = 1.0 / np.abs(powers).max(0)
    fit = np.linalg.lstsq(powers * scale, np.sin(2 * np.pi * nodes), rcond=None)[0]
    return [float(c) for c in fit * scale]


SINE = sine_coefficients()


def sine_turns(turns):
    r = turns - jnp.round(turns)
    s = r * r
    total = jnp.full_like(r, SINE[-1])
    for c in SINE[-2::-1]:
        total = total * s + c
    return total * r


def build_kernel(slab_ref, a_ref, b_ref, c_ref, d_ref, routes_ref, first_ref, second_ref):
    first_ref[0, :512, :] = slab_ref[:, :128]
    first_ref[0, 512:SLAB_ROWS, :] = slab_ref[:, 128:]
    first_ref[0, SLAB_ROWS : SLAB_ROWS + ROUTE_ROWS, :] = routes_ref[...]
    start = SLAB_ROWS + ROUTE_ROWS
    first_ref[0, start : start + TOK, :] = a_ref[...]
    first_ref[0, start + TOK : start + 2 * TOK, :] = b_ref[...]
    second_ref[0, :TOK, :] = c_ref[...]
    last = d_ref[...].astype(f32)
    turned = pltpu.roll(last, 64, 1)
    even = lax.rem(pl.program_id(0), 2) == 0
    low = lax.broadcasted_iota(i32, (128, 128), 1) < 64
    left, right = jnp.where(even, last, turned), jnp.where(even, turned, last)
    second_ref[0, TOK:, :] = jnp.where(low, left[:128], right[128:]).astype(bf16)


def build(tokens, routes_rows):
    return pl.pallas_call(
        build_kernel,
        grid=(EXPERTS,),
        in_specs=[
            pl.BlockSpec((512, TOK), lambda i: (0, 0)),
            pl.BlockSpec((TOK, 128), lambda i: (0, i)),
            pl.BlockSpec((TOK, 128), lambda i: (0, EXPERTS + i)),
            pl.BlockSpec((TOK, 128), lambda i: (0, 2 * EXPERTS + i)),
            pl.BlockSpec((TOK, 128), lambda i: (0, 3 * EXPERTS + i // 2)),
            pl.BlockSpec((ROUTE_ROWS, 128), lambda i: (0, 0)),
        ],
        out_specs=[
            pl.BlockSpec((1, FIRST_ROWS, 128), lambda i: (i, 0, 0)),
            pl.BlockSpec((1, SECOND_ROWS, 128), lambda i: (i, 0, 0)),
        ],
        out_shape=[
            pltpu.HBM((EXPERTS, FIRST_ROWS, 128), bf16),
            pltpu.HBM((EXPERTS, SECOND_ROWS, 128), bf16),
        ],
        compiler_params=pltpu.CompilerParams(vmem_limit_bytes=48 * MIB),
        name="build",
    )(tokens[:, :512].T, *[pltpu.with_memory_space_constraint(tokens, pltpu.HBM)] * 4, routes_rows)


def places_of(routes_rows):
    rows = routes_rows.astype(f32)
    one = jnp.concatenate([rows[0:1], rows[1:2]], axis=1)
    two = jnp.concatenate([rows[2:3], rows[3:4]], axis=1)
    expert = lax.broadcasted_iota(i32, (EXPERTS, TOK), 0).astype(f32)
    member = jnp.where((one == expert) | (two == expert), 1.0, 0.0)
    before = lax.broadcasted_iota(i32, (TOK, TOK), 0) < lax.broadcasted_iota(i32, (TOK, TOK), 1)
    earlier = jnp.dot(
        member.astype(bf16), jnp.where(before, 1.0, 0.0).astype(bf16), preferred_element_type=f32
    )
    return jnp.where(member > 0, earlier, -1.0)


def fill_pick(places, pick_ref, flip):
    slot = lax.broadcasted_iota(i32, (CAP, TOK), 0).astype(f32)
    for e in range(EXPERTS):
        hit = jnp.broadcast_to(places[e : e + 1, :], (CAP, TOK)) == slot
        to = (e ^ flip) * CAP
        pick_ref[to : to + CAP, :] = jnp.where(hit, 1.0, 0.0).astype(bf16)


def split_rows(here_ref, part_ref, keep_ref, send_ref, store):
    x, core = here_ref[0], here_ref[1]
    for step in range(4):
        owner = lax.rem(x + step, 4) * 2
        store(keep_ref, step, part_ref[owner + core])
        store(send_ref, step, part_ref[owner + 1 - core])


def note_largest(top_ref, product):
    largest = jnp.max(jnp.abs(product).reshape(-1, 8, product.shape[1]), axis=0)
    top_ref[...] = jnp.maximum(top_ref[...], jnp.maximum(largest[:, :128], largest[:, 128:]))


def slots_of_pair(pair, blocks, cols, picks, slab, held):
    for source in range(2):
        places = places_of(blocks[source][SLAB_ROWS : SLAB_ROWS + ROUTE_ROWS, :])
        fill_pick(places, picks[source], source)
    low = lax.broadcasted_iota(i32, (512, 128), 1) < CAP
    lanes = pl.ds(pl.multiple_of(pair * 128, 128), 128)
    rows = [jnp.concatenate([block[:512, :], block[512:SLAB_ROWS, :]], axis=1) for block in blocks]
    for quarter in range(4):
        got = [
            lax.dot_general(
                rows[source],
                picks[source][quarter * 256 : (quarter + 1) * 256, :],
                (((1,), (1,)), ((), ())),
                preferred_element_type=f32,
            ).astype(bf16)
            for source in range(2)
        ]
        for half in range(2):
            m = 2 * quarter + half
            a, b = (g[:, half * 128 : (half + 1) * 128] for g in got)
            slab[2 * m, :, lanes] = jnp.where(low, a, b)
            slab[2 * m + 1, :, lanes] = jnp.where(low, b, a)
    for quarter in range(4):
        got = [
            jnp.dot(
                picks[source][quarter * 256 : (quarter + 1) * 256, :],
                cols[source],
                preferred_element_type=f32,
            ).astype(bf16)
            for source in range(2)
        ]
        for source in range(2):
            for block in range(4):
                e = (4 * quarter + block) ^ source
                offset = CAP * ((e + source) % 2)
                held[e, pl.ds(pl.multiple_of(pair * 128 + offset, CAP), CAP), :] = got[source][
                    block * CAP : (block + 1) * CAP
                ]


def product0_kernel(here_ref, in_ref, keep_ref, send_ref, top_ref, pick0, pick1, slab, held, part):
    step = pl.program_id(0)

    @pl.when(step == 0)
    def _():
        top_ref[...] = jnp.zeros_like(top_ref)

    @pl.when(step < 8)
    def _():
        blocks = [in_ref.at[source] for source in range(2)]
        start = SLAB_ROWS + ROUTE_ROWS
        cols = [
            jnp.concatenate(
                [block[start : start + TOK, :], block[start + TOK : start + 2 * TOK, :]], axis=1
            )
            for block in blocks
        ]
        slots_of_pair(step, blocks, cols, (pick0, pick1), slab, held)

    @pl.when(step >= 8)
    def _():
        products = [
            jnp.dot(slab[e], held[e], preferred_element_type=f32)
            for e in (2 * (step - 8), 2 * (step - 8) + 1)
        ]
        for k in range(2):
            note_largest(top_ref, products[k])
            part[k] = products[k].reshape(8, 64, 256)
        for k in range(2):

            def store(ref, at, value):
                ref[at, k * 64 : (k + 1) * 64] = value

            split_rows(here_ref, part.at[k], keep_ref, send_ref, store)


SCRATCH = [
    pltpu.VMEM((1024, TOK), bf16),
    pltpu.VMEM((1024, TOK), bf16),
    pltpu.VMEM((EXPERTS, 512, 1024), bf16),
    pltpu.VMEM((EXPERTS, 1024, 256), bf16),
    pltpu.VMEM((2, 8, 64, 256), f32),
]


def early(i, here):
    return (jnp.minimum(i, 7), 0, 0)


def product0(here, first):
    rows = pl.BlockSpec((4, 128, 256), lambda i, here: (0, jnp.maximum(i - 8, 0), 0))
    return pl.pallas_call(
        product0_kernel,
        grid_spec=pltpu.PrefetchScalarGridSpec(
            num_scalar_prefetch=1,
            grid=(16,),
            in_specs=[pl.BlockSpec((2, FIRST_ROWS, 128), early)],
            out_specs=[rows, rows, pl.BlockSpec((8, 128), lambda i, here: (0, 0))],
            scratch_shapes=SCRATCH,
        ),
        out_shape=[pltpu.HBM((4, EXPERTS * 64 + EXTRA, 256), f32)] * 2
        + [jax.ShapeDtypeStruct((8, 128), f32)],
        compiler_params=pltpu.CompilerParams(vmem_limit_bytes=40 * MIB),
        cost_estimate=pl.CostEstimate(flops=11 * 10**9, bytes_accessed=16 * 10**6, transcendentals=0),
        name="product0",
    )(here, first)


def product1_kernel(
    here_ref, in_ref, cols_ref, keep_ref, send_ref, top_ref, pick0, pick1, slab, held, part
):
    step = pl.program_id(0)

    @pl.when(step == 0)
    def _():
        top_ref[...] = jnp.zeros_like(top_ref)

    @pl.when(step < 8)
    def _():
        blocks = [in_ref.at[source] for source in range(2)]
        cols = []
        for source in range(2):
            last = cols_ref[source, TOK:, :]
            turned = pltpu.roll(last.astype(f32), 64, 1).astype(bf16)
            last = jnp.concatenate([last, turned], axis=0)
            cols.append(jnp.concatenate([cols_ref[source, :TOK, :], last], axis=1))
        slots_of_pair(step, blocks, cols, (pick0, pick1), slab, held)

    @pl.when(step >= 8)
    def _():
        experts = (2 * (step - 8), 2 * (step - 8) + 1)
        products = [jnp.dot(slab[e], held[e], preferred_element_type=f32) for e in experts]
        for k in range(2):
            note_largest(top_ref, products[k])
            part[k] = products[k].reshape(8, 64, 256)
        for k in range(2):

            def store(ref, at, value):
                ref[at, pl.ds(pl.multiple_of(experts[k] * 64, 64), 64)] = value[:, :128]

            split_rows(here_ref, part.at[k], keep_ref, send_ref, store)

        low = lax.broadcasted_iota(i32, (512, 128), 1) < 64
        both = jnp.where(low, products[0][:, 128:], pltpu.roll(products[1][:, 128:], 64, 1))
        part[0, :, :, :128] = both.reshape(8, 64, 128)

        def store_last(ref, at, value):
            start = EXPERTS * 64 + (step - 8) * 64
            ref[at, pl.ds(pl.multiple_of(start, 64), 64)] = value[:, :128]

        split_rows(here_ref, part.at[0], keep_ref, send_ref, store_last)


def product1(here, first, second):
    rows = pl.BlockSpec(
        (4, 24 * 64 + EXTRA, 128), lambda i, here: (0, 0, 0), pipeline_mode=pl.Buffered(1)
    )
    return pl.pallas_call(
        product1_kernel,
        grid_spec=pltpu.PrefetchScalarGridSpec(
            num_scalar_prefetch=1,
            grid=(16,),
            in_specs=[
                pl.BlockSpec((2, FIRST_ROWS, 128), early),
                pl.BlockSpec((2, SECOND_ROWS, 128), early),
            ],
            out_specs=[rows, rows, pl.BlockSpec((8, 128), lambda i, here: (0, 0))],
            scratch_shapes=SCRATCH,
        ),
        out_shape=[pltpu.HBM((4, 24 * 64 + EXTRA, 128), f32)] * 2
        + [jax.ShapeDtypeStruct((8, 128), f32)],
        compiler_params=pltpu.CompilerParams(vmem_limit_bytes=44 * MIB),
        cost_estimate=pl.CostEstimate(flops=11 * 10**9, bytes_accessed=16 * 10**6, transcendentals=0),
        name="product1",
    )(here, first, second)


def sum_over_core(keep, send, top):
    other = lax.ppermute(send, "core", SWAP)
    top = jnp.max(top) + jnp.max(lax.ppermute(top, "core", SWAP))
    exponent = jnp.clip(jnp.floor(jnp.log2(32000.0 / jnp.maximum(top, 1e-30))), -100.0, 100.0)
    factor = jnp.exp2(exponent)
    rows = keep.shape[1] - EXTRA
    value = lax.broadcasted_iota(i32, keep.shape[1:], 0) < rows
    others = [
        jnp.where(value, (keep[i] + other[i]) * factor, exponent).astype(f16) for i in (1, 2, 3)
    ]
    return (keep[0], other[0]), others


def sum_over_x(own, others):
    rows = own[0].shape[0] - EXTRA

    def wide(value):
        return value.astype(f32) * jnp.exp2(-value[rows : rows + 1].astype(f32))

    one, two, three = others
    return ((own[0] + own[1] + wide(two)) + (wide(one) + wide(three)))[:rows]


def over_x(others):
    return [lax.ppermute(value, "x", pairs) for value, pairs in zip(others, (UP, OPPOSITE, DOWN))]


def over_dp(value):
    a, b, c = (lax.ppermute(value, "x", pairs) for pairs in (UP, OPPOSITE, DOWN))
    value = (value + b) + (a + c)
    return value + lax.ppermute(value, "core", SWAP)


def order_kernel(half_ref, scale_ref, a_ref, b_ref, out_ref):
    scale = scale_ref[0]
    half = half_ref[0]
    for i in range(EXPERTS):
        out_ref[:, i * 128 : (i + 1) * 128] = a_ref[i, :, :128] * scale
        out_ref[:, (16 + i) * 128 : (17 + i) * 128] = a_ref[i, :, 128:] * scale
        out_ref[:, (32 + i) * 128 : (33 + i) * 128] = b_ref[i, :64, :] * scale
    low = lax.broadcasted_iota(i32, (64, 128), 1) < 64
    for t in range(8):
        left, right = b_ref[2 * t, 64:, :], b_ref[2 * t + 1, 64:, :]
        even = jnp.where(low, left, pltpu.roll(right, 64, 1))
        odd = jnp.where(low, pltpu.roll(left, 64, 1), right)
        out_ref[:, (48 + t) * 128 : (49 + t) * 128] = jnp.where(half == 0, even, odd) * scale


def put_in_order(half, scale, a, b):
    smem, vmem = pl.BlockSpec(memory_space=pltpu.SMEM), pl.BlockSpec(memory_space=pltpu.VMEM)
    return pl.pallas_call(
        order_kernel,
        in_specs=[smem, smem, vmem, vmem],
        out_specs=vmem,
        out_shape=jax.ShapeDtypeStruct((64, 7168), f32),
        compiler_params=pltpu.CompilerParams(vmem_limit_bytes=16 * MIB),
        name="put_in_order",
    )(half, scale, a, b)


def columns_kernel(block_ref, levels_ref, pivots_ref, upper_ref, turned_ref, snapped_ref, errors_ref, now, out, err):
    block = block_ref[...].astype(f32).T
    now[...] = block
    largest = jnp.max(jnp.abs(block), axis=0, keepdims=True)
    spacing = (largest + 1e-05) / levels_ref[...].astype(f32)
    per_turn = 1.0 / spacing
    reach = 0.9 * spacing / (2.0 * math.pi)
    lane = lax.broadcasted_iota(i32, (8, BLOCK), 1)

    def group(b, carry):
        at = pl.multiple_of(b * 8, 8)
        tile = now[pl.ds(at, 8), :]
        turned = turned_ref[pl.ds(at, 8), :]
        near = [
            jnp.sum(jnp.where(lane == at + i, turned, 0.0), axis=1, keepdims=True) for i in range(8)
        ]
        snapped, errors = [], []
        for i in range(8):
            values = tile[i : i + 1, :]
            moved = values - reach * sine_turns(values * per_turn)
            error = (values - moved) * pivots_ref[at + i]
            tile = tile - near[i] * error
            snapped.append(moved)
            errors.append(error)
        errors = jnp.concatenate(errors, axis=0)
        out[pl.ds(at, 8), :] = jnp.concatenate(snapped, axis=0)
        err[pl.ds(at, 8), :] = errors
        now[...] -= lax.dot_general(
            upper_ref[pl.ds(at, 8), :],
            errors,
            (((0,), (0,)), ((), ())),
            precision=lax.Precision.HIGHEST,
            preferred_element_type=f32,
        )
        return carry

    lax.fori_loop(0, BLOCK // 8, group, 0)
    snapped_ref[...] = out[...].T
    errors_ref[...] = err[...].T


def block_update(rows, levels, pivots, upper):
    whole = lambda *shape: pl.BlockSpec(shape, lambda i: (0,) * len(shape))
    count = rows.shape[0]
    return pl.pallas_call(
        columns_kernel,
        grid=(1,),
        in_specs=[
            whole(count, BLOCK),
            whole(1, count),
            pl.BlockSpec(memory_space=pltpu.SMEM),
            whole(BLOCK, BLOCK),
            whole(BLOCK, BLOCK),
        ],
        out_specs=[whole(count, BLOCK)] * 2,
        out_shape=[jax.ShapeDtypeStruct((count, BLOCK), f32)] * 2,
        scratch_shapes=[pltpu.VMEM((BLOCK, count), f32)] * 3,
        compiler_params=pltpu.CompilerParams(vmem_limit_bytes=16 * MIB),
        cost_estimate=pl.CostEstimate(flops=10**9, bytes_accessed=2 * 10**6, transcendentals=0),
        name="block_update",
    )(rows, levels, 1.0 / pivots, upper, upper.T)


def panel_over_x(panel):
    mine = panel.T.astype(bf16)
    return [mine] + [lax.ppermute(mine, "x", pairs) for pairs in (DOWN, OPPOSITE, UP)]


def whole_panel(ahead, x, first):
    other = list(lax.ppermute(jnp.stack(ahead), "core", SWAP))
    pieces = []
    for at in range(4):
        mine, theirs = (lax.select_n(lax.rem(at + 4 - x, 4), *parts) for parts in (ahead, other))
        pieces += [jnp.where(first, mine, theirs), jnp.where(first, theirs, mine)]
    return jnp.concatenate(pieces, axis=0)


def later_kernel(errors_ref, panel_ref, *refs):
    *weight_refs, out_ref, done_ref = refs
    errors = errors_ref[...]
    panel = panel_ref[...]
    total = None
    for _ in range(3):
        part = errors.astype(bf16)
        errors = errors - part.astype(f32)
        product = lax.dot_general(part, panel, (((1,), (1,)), ((), ())), preferred_element_type=f32)
        total = product if total is None else total + product
    for k, ref in enumerate(weight_refs):
        out_ref[:, k * 128 : (k + 1) * 128] = ref[...].astype(f32) - total[:, k * 128 : (k + 1) * 128]
    done_ref[...] = jnp.zeros_like(done_ref)


def later_columns(rows, errors, panel):
    count, later = rows.shape[0], panel.shape[0]
    columns = [
        pl.BlockSpec((count, 128), functools.partial(lambda k, i: (0, 5 * i + k), k)) for k in range(1, 6)
    ]
    return pl.pallas_call(
        later_kernel,
        grid=(later // 640,),
        in_specs=[
            pl.BlockSpec((count, BLOCK), lambda i: (0, 0)),
            pl.BlockSpec((640, BLOCK), lambda i: (i, 0)),
        ]
        + columns,
        out_specs=[
            pl.BlockSpec((count, 640), lambda i: (0, i)),
            pl.BlockSpec((8, 128), lambda i: (0, 0)),
        ],
        out_shape=[pltpu.HBM((count, later), f32), jax.ShapeDtypeStruct((8, 128), f32)],
        compiler_params=pltpu.CompilerParams(vmem_limit_bytes=16 * MIB),
        cost_estimate=pl.CostEstimate(flops=15 * 10**8, bytes_accessed=13 * 10**6, transcendentals=0),
        name="later_columns",
    )(errors, panel, *[rows] * 5)


def on_device(tokens, routes, weight, levels, pivots, panel_diag, panel_rest):
    x, core = lax.axis_index("x"), lax.axis_index("core")
    place = lax.axis_index("z") * 4 + lax.axis_index("y")
    routes_rows = jnp.pad(routes.T.reshape(4, 128).astype(bf16), ((0, ROUTE_ROWS - 4), (0, 0)))
    exchange = functools.partial(
        lax.all_to_all, axis_name=PLANE, split_axis=0, concat_axis=0, tiled=True
    )
    here = jnp.stack([x, core]).astype(i32)
    half = lax.rem(place, 2).astype(i32)[None]
    first_core = core == 0

    first, second = build(tokens, routes_rows)
    first, here, half, place, x, first_core, pivots = lax.optimization_barrier(
        (first, here, half, place, x, first_core, pivots)
    )
    first = exchange(first)
    first, second, weight, levels, panel_diag, panel_rest, pivots = lax.optimization_barrier(
        (first, second, weight, levels, panel_diag, panel_rest, pivots)
    )
    second = exchange(second)
    keep, send, top = product0(here, first)
    send, top, second, weight, panel_rest = lax.optimization_barrier(
        (send, top, second, weight, panel_rest)
    )
    own, others = sum_over_core(keep, send, top)

    rows = weight[0]
    upper = jnp.triu(panel_diag[0], 1)
    snapped, errors = block_update(rows, levels, pivots[0], upper)
    panel = panel_over_x(panel_rest[0])

    first, second, others, panel, errors = lax.optimization_barrier(
        (first, second, others, panel, errors)
    )
    others = over_x(others)
    keep, send, top = product1(here, first, second)
    keep, send, top, others, rows, panel, first = lax.optimization_barrier(
        (keep, send, top, others, rows, panel, first)
    )
    total = exchange(sum_over_x(own, others).reshape(EXPERTS, 64, 256))
    own, others = sum_over_core(keep, send, top)

    others, rows, errors, panel, first = lax.optimization_barrier((others, rows, errors, panel, first))
    others = over_x(others)
    remainder, done = later_columns(rows, errors, whole_panel(panel, x, first_core))
    others, done = lax.optimization_barrier((others, done))

    named = first[:, SLAB_ROWS : SLAB_ROWS + 4, :].reshape(1, -1).astype(f32)
    counts = jnp.sum(
        (named == lax.broadcasted_iota(i32, (EXPERTS, 1), 0).astype(f32)).astype(f32), axis=1
    )
    counts = over_dp(jnp.broadcast_to(jnp.pad(counts, (0, 128 - EXPERTS)), (8, 128)))[0]
    own_count = lax.dynamic_index_in_dim(counts, place, 0, keepdims=True)

    tail = sum_over_x(own, others).reshape(24, 64, 128)
    tail = exchange(
        jnp.concatenate([tail[:EXPERTS], jnp.repeat(tail[EXPERTS:], 2, axis=0)], axis=1)
    )
    hessian = put_in_order(half, 2.0 / own_count, total, tail)
    return hessian[None], snapped[None], remainder[None]


def solution(mesh):
    devices = mesh.devices
    fine = Mesh(devices.reshape(4, 2, 4, 4), ("x", "core", "z", "y"))
    dp, every = ("x", "core"), ("x", "core", "z", "y")
    return jax.shard_map(
        on_device,
        mesh=fine,
        in_specs=(
            P(every, None),
            P(every, None),
            P(PLANE, dp, None),
            P(PLANE, dp),
            P(PLANE, None),
            P(PLANE, None, None),
            P(PLANE, None, dp),
        ),
        out_specs=(P(PLANE, dp, None),) * 3,
        check_vma=False,
    )
```

time: 581 us -> 251 us (0.43)
  waiting for transfers between devices: 215 us -> 18.8 us
  local copies, waits for them, and re-layouts: 123 us -> 9.24 us
  other arithmetic: 124 us -> 27.7 us
  Pallas kernels: 0 us -> 73.3 us
  starting transfers between devices: 8.31 us -> 33.8 us
  matrix products: 22.1 us -> 0 us
  blocking collectives: 62.6 us -> 82.2 us
  between operations: 14.9 us -> 3.91 us
    all_to_all x1 -> x3, waiting for transfers between devices: 215 us -> 3.29 us  [the longest x1 3.04 us: on_device(): exchange(jnp.concatenate([tail[:EXPERTS], jnp.repeat(tail[EXPERTS:], 2, a...]
    div x129 -> x2, other arithmetic: 90.4 us -> 0.63 us  [the longest x1 0.62 us: on_device(): hessian = put_in_order(half, 2.0 / own_count, total, tail)]
    all_to_all x0 -> x1, blocking collectives: none -> 82.2 us  [on_device(): first = exchange(first)]
    dynamic_slice x128 -> x0, local copies, waits for them, and re-layouts: 75 us -> none  [advance(): lax.dynamic_slice_in_dim(pivots, column, 1, 0)[None, :]]
    pallas_call x0 -> x6, Pallas kernels: none -> 73.3 us  [the longest x1 20.7 us: product1(): pl.pallas_call(product1_kernel, grid_spec=pltpu.PrefetchScalarGridSpec(nu...]
    psum x1 -> x0, blocking collectives: 62.6 us -> none  [on_device(): totals = lax.psum(local_counts, ('dp', 'expert'))]
    gather x1 -> x0, local copies, waits for them, and re-layouts: 27.3 us -> none  [on_device(): tokens[slot_source]]
    dot_general x2 -> x0, matrix products: 22.1 us -> none  [the longest x1 14.7 us: on_device(): jnp.einsum('tr,tc->rc', received[:, :HROWS], received, preferred_element_...]
  transfers between devices with their start and end apart: 3 -> 21, of which waited for: 1 -> 8; matrix products, arithmetic and copies ran while one was open for 37% -> 9% of each run, Pallas kernels for 0% -> 24%
where the time goes in v1:
time: 251 us; the launch traced here: 249 us
  blocking collectives  82.2 us (33%)
  Pallas kernels  73.3 us (29%)
  starting transfers between devices  33.8 us (13%)
  other arithmetic  27.7 us (11%)
  waiting for transfers between devices  18.8 us (7%)
  local copies, waits for them, and re-layouts  9.24 us (4%)
  between operations  3.91 us (2%)
    all_to_all x1, blocking collectives, on_device(): first = exchange(first)  82.2 us
    pallas_call x1, Pallas kernels, product1(): pl.pallas_call(product1_kernel, grid_spec=pltpu.PrefetchScalarGridSpec(nu...  20.7 us
    pallas_call x1, Pallas kernels, product0(): pl.pallas_call(product0_kernel, grid_spec=pltpu.PrefetchScalarGridSpec(nu...  19.5 us
    ppermute x6, waiting for transfers between devices, over_x(): lax.ppermute(value, 'x', pairs)  12.9 us
    pallas_call x1, Pallas kernels, build(): pl.pallas_call(build_kernel, grid=(EXPERTS,), in_specs=[pl.BlockSpec((512...  11 us
    pallas_call x1, Pallas kernels, later_columns(): pl.pallas_call(later_kernel, grid=(later // 640,), in_specs=[pl.BlockSpec...  10.2 us
    pallas_call x1, Pallas kernels, block_update(): pl.pallas_call(columns_kernel, grid=(1,), in_specs=[whole(count, BLOCK),...  9.76 us
    ppermute x6, starting transfers between devices, over_x(): lax.ppermute(value, 'x', pairs)  9.28 us
  transfers between devices with their start and end apart: 21, of which 8 were waited for; matrix products, arithmetic and copies ran while one was open for 9% of the time, Pallas kernels for 24%

profile of v1, /device:TPU:6, one launch (start us, length us, event | category | flops | bytes accessed | tf_op | source)
XLA Modules:
  0.0 249.0 jit_solution(11989677775834208336)
XLA Ops:
  2.5 11.0 %build.1 = (bf16[16,1552,128]{2,1,0:T(8,128)(2,1)}, bf16[16,384,128]{2,1,0:T(8,128)(2,1)}) custom-call(bf16[512,256]{1,0:T(8,128)(2,1)S(1)} %bitcast.122, bf16[256,7168]{1,0:T(8,128)(2,1)} %d_ref.1, bf16[256,7168]{1,0:T(8,128)(2,1)} %d_ref.1, bf16[256,7168]{1,0:T(8,128)(2,1)} %d_ref.1, bf16[256,7168]{1,0:T(8,128)(2,1)} %d_ref.1, ...), custom_call_target="tpu_custom_call" | custom-call | tf_op jit(solution)/shard_map/build/pallas_call | solution.py:67
  13.5 82.2 %all_to_all.20.in_ref = bf16[16,1552,128]{2,1,0:T(8,128)(2,1)} all-to-all(bf16[16,1552,128]{2,1,0:T(8,128)(2,1)} %get-tuple-element.71), channel_id=1, replica_groups=mesh['x'=4,'core'=2,'z'=4,'y'=4] {'z','y'}, dimensions={0} | all-to-all | bytes 12713984 | tf_op jit(solution)/shard_map/all_to_all | solution.py:493
  95.7 3.7 %all-to-all-start.1 = ((bf16[16,384,128]{2,1,0:T(8,128)(2,1)}), bf16[16,384,128]{2,1,0:T(8,128)(2,1)S(1)}, u32[]{:S(2)}, u32[]{:S(2)}) async-start(bf16[16,384,128]{2,1,0:T(8,128)(2,1)} %get-tuple-element.77), calls=%async_computation.1 | async-start | bytes 3145728 | tf_op jit(solution)/shard_map/all_to_all | solution.py:497
  99.5 2.8 %copy-done.2 = bf16[16,1552,128]{2,1,0:T(8,128)(2,1)S(1)} copy-done((bf16[16,1552,128]{2,1,0:T(8,128)(2,1)S(1)}, bf16[16,1552,128]{2,1,0:T(8,128)(2,1)}, u32[]{:S(2)}) %copy-start.2) | copy-done | bytes 6357016
  102.3 19.5 %product0.1 = (f32[4,1040,256]{2,1,0:T(8,128)}, f32[4,1040,256]{2,1,0:T(8,128)}, f32[8,128]{1,0:T(8,128)S(1)}) custom-call(s32[2]{0:T(128)S(1)} %pad_add_fusion.here_ref, bf16[16,1552,128]{2,1,0:T(8,128)(2,1)S(1)} %copy-done.2), custom_call_target="tpu_custom_call" | custom-call | flops 11000000512 | bytes 16000000 | tf_op jit(solution)/shard_map/product0/pallas_call | solution.py:216
  122.0 1.1 copy-done.3
  124.0 2.4 collective-permute-start.3
  126.4 2.0 copy-done
  128.5 9.8 %block_update.1 = (f32[256,128]{1,0:T(8,128)}, f32[256,128]{1,0:T(8,128)S(1)}) custom-call(bf16[256,7168]{1,0:T(8,128)(2,1)S(1)} %bitcast.114, s32[1,256]{1,0:T(1,128)S(1)} %copy-done.5, f32[128]{0:T(128)S(1)} %divide_bitcast_fusion.pivots_ref, f32[128,128]{1,0:T(8,128)S(1)} %copy.15.upper_ref, f32[128,128]{1,0:T(8,128)S(1)} %get-tuple-element.151.turned_ref), custom_call_target="tpu_custom_call" | custom-call | flops 1000000000 | bytes 2000000 | tf_op jit(solution)/shard_map/block_update/pallas_call | solution.py:406
  140.9 3.5 %fusion.4 = (f16[1040,256]{1,0:T(8,128)(2,1)S(1)}, f16[1040,256]{1,0:T(8,128)(2,1)S(1)}, f16[1040,256]{1,0:T(8,128)(2,1)S(1)}) fusion(f32[4,1040,256]{2,1,0:T(8,128)} %collective-permute-done, f32[4,1040,256]{2,1,0:T(8,128)} %get-tuple-element.81, f32[]{:T(128)S(6)} %min.7, f32[]{:T(128)S(6)} %exp2.49, pred[1040]{0:T(1024)(128)(4,1)S(1)} %iota_compare_fusion.1), kind=kLoop, calls=%fused_computation.6 | loop fusion | flops 3194880 | bytes 7988248 | tf_op jit(solution)/shard_map/convert_element_type | solution.py:310
  144.5 3.3 %collective-permute-start.5 = (f16[1040,256]{1,0:T(8,128)(2,1)S(1)}, f16[1040,256]{1,0:T(8,128)(2,1)S(1)}, u32[]{:S(2)}, u32[]{:S(2)}) collective-permute-start(f16[1040,256]{1,0:T(8,128)(2,1)S(1)} %get-tuple-element.95), channel_id=1, source_target_pairs={{0,32},{32,64},{64,96},{96,0},{1,33},{33,65},{65,97},{97,1},{2,34}... | collective-permute-start | bytes 1597448 | tf_op jit(solution)/shard_map/ppermute | solution.py:326
  147.9 1.3 collective-permute-start.7
  149.3 20.7 %product1.1 = (f32[4,1552,128]{2,1,0:T(8,128)}, f32[4,1552,128]{2,1,0:T(8,128)}, f32[8,128]{1,0:T(8,128)S(1)}) custom-call(s32[2]{0:T(128)S(1)} %pad_add_fusion.here_ref, bf16[16,1552,128]{2,1,0:T(8,128)(2,1)S(1)} %bitcast.121, bf16[16,384,128]{2,1,0:T(8,128)(2,1)S(1)} %copy-done.4), custom_call_target="tpu_custom_call" | custom-call | flops 11000000512 | bytes 16000000 | tf_op jit(solution)/shard_map/product1/pallas_call | solution.py:282
  170.0 1.3 collective-permute-done.5
  171.2 3.5 %collective-permute-done.7 = f16[1040,256]{1,0:T(8,128)(2,1)S(1)} collective-permute-done((f16[1040,256]{1,0:T(8,128)(2,1)S(1)}, f16[1040,256]{1,0:T(8,128)(2,1)S(1)}, u32[]{:S(2)}, u32[]{:S(2)}) %collective-permute-start.7) | collective-permute-done | bytes 532512 | tf_op jit(solution)/shard_map/ppermute | solution.py:326
  175.6 1.7 fusion
  179.2 2.1 collective-permute-done.9
  183.4 3.7 %fusion.20 = (f16[1552,128]{1,0:T(8,128)(2,1)}, f16[1552,128]{1,0:T(8,128)(2,1)}, f16[1552,128]{1,0:T(8,128)(2,1)}) fusion(f32[4,1552,128]{2,1,0:T(8,128)} %collective-permute-done.8, f32[4,1552,128]{2,1,0:T(8,128)} %get-tuple-element.102, f32[]{:T(128)S(6)} %min.8, f32[]{:T(128)S(6)} %exp2.51, pred[1552]{0:T(1024)(128)(4,1)S(1)} %iota_compare_fusion.2), kind=kLoop, calls=%fused_computation.29 | loop fusion | flops 2383872 | bytes 5961240 | tf_op jit(solution)/shard_map/convert_element_type | solution.py:310
  189.2 1.1 collective-permute-start.12
  190.9 2.2 collective-permute-start.14
  193.1 2.3 collective-permute-start.15
  195.5 1.4 fusion.13
  196.9 6.9 %all-to-all-start.2 = ((f32[16,64,256]{2,1,0:T(8,128)}), f32[16,64,256]{2,1,0:T(8,128)S(1)}, u32[]{:S(2)}, u32[]{:S(2)}) async-start(f32[16,64,256]{2,1,0:T(8,128)} %bitcast.24), calls=%async_computation.2 | async-start | bytes 2097152 | tf_op jit(solution)/shard_map/all_to_all | solution.py:517
  205.7 4.5 %collective-permute-done.14 = f16[1552,128]{1,0:T(8,128)(2,1)} collective-permute-done((f16[1552,128]{1,0:T(8,128)(2,1)}, f16[1552,128]{1,0:T(8,128)(2,1)}, u32[]{:S(2)}, u32[]{:S(2)}) %collective-permute-start.14) | collective-permute-done | bytes 397344 | tf_op jit(solution)/shard_map/ppermute | solution.py:326
  210.2 3.6 %collective-permute-done.16 = f16[1552,128]{1,0:T(8,128)(2,1)} collective-permute-done((f16[1552,128]{1,0:T(8,128)(2,1)}, f16[1552,128]{1,0:T(8,128)(2,1)}, u32[]{:S(2)}, u32[]{:S(2)}) %collective-permute-start.16) | collective-permute-done | bytes 397344 | tf_op jit(solution)/shard_map/ppermute | solution.py:326
  215.2 2.0 fusion.16
  217.4 1.1 pad_maximum_fusion
  222.1 6.9 %all-to-all-start.3 = ((f32[16,128,128]{2,1,0:T(8,128)}), f32[16,128,128]{2,1,0:T(8,128)S(1)}, u32[]{:S(2)}, u32[]{:S(2)}) async-start(f32[16,128,128]{2,1,0:T(8,128)} %pad_maximum_fusion), calls=%async_computation.3 | async-start | bytes 2097152 | tf_op jit(solution)/shard_map/all_to_all | solution.py:533
  229.1 2.1 fusion.31
  233.6 10.2 %later_columns.1 = (f32[256,7040]{1,0:T(8,128)}, f32[8,128]{1,0:T(8,128)}) custom-call(f32[256,128]{1,0:T(8,128)S(1)} %get-tuple-element.124.errors_ref, bf16[7040,128]{1,0:T(8,128)(2,1)} %fusion.30.panel_ref, bf16[256,7168]{1,0:T(8,128)(2,1)S(1)} %bitcast.115, bf16[256,7168]{1,0:T(8,128)(2,1)S(1)} %bitcast.116, bf16[256,7168]{1,0:T(8,128)(2,1)S(1)} %bitcast.117, ...), custom_call_target="tpu_custom_call" | custom-call | flops 1500000000 | bytes 13000000 | tf_op jit(solution)/shard_map/later_columns/pallas_call | solution.py:459
  243.8 3.0 %all-to-all-done.3.b_ref = f32[16,128,128]{2,1,0:T(8,128)S(1)} async-done(((f32[16,128,128]{2,1,0:T(8,128)}), f32[16,128,128]{2,1,0:T(8,128)S(1)}, u32[]{:S(2)}, u32[]{:S(2)}) %all-to-all-start.3) | async-done | bytes 1048608 | tf_op jit(solution)/shard_map/all_to_all | solution.py:533
  246.8 2.2 put_in_order.1
  (119 shorter events, 19.8 us)
Async XLA Ops:
  95.7 26.3 %all-to-all-start.1 = ((bf16[16,384,128]{2,1,0:T(8,128)(2,1)}), bf16[16,384,128]{2,1,0:T(8,128)(2,1)S(1)}, u32[]{:S(2)}, u32[]{:S(2)}) async-start(bf16[16,384,128]{2,1,0:T(8,128)(2,1)} %get-tuple-element.77), calls=%async_computation.1 | async-start | bytes 3145728 | tf_op jit(solution)/shard_map/all_to_all | solution.py:497
  102.3 20.9 %copy-start.22 = (f32[1,128,128]{2,1,0:T(8,128)S(1)}, f32[1,128,128]{2,1,0:T(8,128)}, u32[]{:S(2)}) copy-start(f32[1,128,128]{2,1,0:T(8,128)} %param.12) | copy-start | bytes 196612
  102.3 21.1 %copy-start.23 = (f32[1,128]{1,0:T(1,128)S(1)}, f32[1,128]{1,0:T(1,128)}, u32[]{:S(2)}) copy-start(f32[1,128]{1,0:T(1,128)} %param.11) | copy-start | bytes 1540
  102.3 21.1 %copy-start.21 = (f32[1,128,880]{1,2,0:T(8,128)S(1)}, f32[1,128,880]{1,2,0:T(8,128)}, u32[]{:S(2)}) copy-start(f32[1,128,880]{1,2,0:T(8,128)} %param.13) | copy-start | bytes 1351684
  102.3 24.1 %copy-start.5 = (s32[1,256]{1,0:T(1,128)S(1)}, s32[1,256]{1,0:T(1,128)}, u32[]{:S(2)}) copy-start(s32[1,256]{1,0:T(1,128)} %levels_ref) | copy-start | bytes 3076
  123.1 17.8 %collective-permute-start = (f32[4,1040,256]{2,1,0:T(8,128)}, f32[4,1040,256]{2,1,0:T(8,128)}, u32[]{:S(2)}, u32[]{:S(2)}) collective-permute-start(f32[4,1040,256]{2,1,0:T(8,128)} %get-tuple-element.82), channel_id=1, source_target_pairs={{0,16},{16,0},{1,17},{17,1},{2,18},{18,2},{3,19},{19,3},{4,20},{20... | collective-permute-start | bytes 12779528 | tf_op jit(solution)/shard_map/ppermute | solution.py:303
  123.4 21.0 %collective-permute-start.4 = (bf16[880,128]{1,0:T(8,128)(2,1)S(1)}, bf16[880,128]{1,0:T(8,128)(2,1)S(1)}, u32[]{:S(2)}, u32[]{:S(2)}) collective-permute-start(bf16[880,128]{1,0:T(8,128)(2,1)S(1)} %convert_bitcast_fusion), channel_id=1, source_target_pairs={{0,32},{32,64},{64,96},{96,0},{1,33},{33,65},{65,97},{97,1},{2,34}... | collective-permute-start | bytes 675848 | tf_op jit(solution)/shard_map/ppermute | solution.py:427
  124.0 20.5 %collective-permute-start.3 = (bf16[880,128]{1,0:T(8,128)(2,1)S(1)}, bf16[880,128]{1,0:T(8,128)(2,1)S(1)}, u32[]{:S(2)}, u32[]{:S(2)}) collective-permute-start(bf16[880,128]{1,0:T(8,128)(2,1)S(1)} %convert_bitcast_fusion), channel_id=1, source_target_pairs={{0,64},{32,96},{64,0},{96,32},{1,65},{33,97},{65,1},{97,33},{2,66}... | collective-permute-start | bytes 675848 | tf_op jit(solution)/shard_map/ppermute | solution.py:427
  126.4 18.1 %collective-permute-start.2 = (bf16[880,128]{1,0:T(8,128)(2,1)S(1)}, bf16[880,128]{1,0:T(8,128)(2,1)S(1)}, u32[]{:S(2)}, u32[]{:S(2)}) collective-permute-start(bf16[880,128]{1,0:T(8,128)(2,1)S(1)} %convert_bitcast_fusion), channel_id=1, source_target_pairs={{0,96},{32,0},{64,32},{96,64},{1,97},{33,1},{65,33},{97,65},{2,98}... | collective-permute-start | bytes 675848 | tf_op jit(solution)/shard_map/ppermute | solution.py:427
  126.4 12.4 %collective-permute-start.1 = (f32[8,128]{1,0:T(8,128)S(1)}, f32[8,128]{1,0:T(8,128)S(1)}, u32[]{:S(2)}, u32[]{:S(2)}) collective-permute-start(f32[8,128]{1,0:T(8,128)S(1)} %get-tuple-element.83), channel_id=1, source_target_pairs={{0,16},{16,0},{1,17},{17,1},{2,18},{18,2},{3,19},{19,3},{4,20},{20... | collective-permute-start | bytes 12296 | tf_op jit(solution)/shard_map/ppermute | solution.py:304
  128.5 20.8 %slice-start = ((s8[6356992]{0:T(1024)(128)(4,1)}), s8[2162688]{0:T(1024)(128)(4,1)S(1)}, s32[]{:S(2)}) async-start(s8[6356992]{0:T(1024)(128)(4,1)} %bitcast.120), calls=%async_computation.4 | async-start | bytes 4325376
  140.9 8.3 %slice-start.1 = ((s8[6356992]{0:T(1024)(128)(4,1)}), s8[4194304]{0:T(1024)(128)(4,1)S(1)}, s32[]{:S(2)}) async-start(s8[6356992]{0:T(1024)(128)(4,1)} %bitcast.120), calls=%async_computation.5 | async-start | bytes 8388608
  140.9 8.3 %copy-start.4 = (bf16[16,384,128]{2,1,0:T(8,128)(2,1)S(1)}, bf16[16,384,128]{2,1,0:T(8,128)(2,1)}, u32[]{:S(2)}) copy-start(bf16[16,384,128]{2,1,0:T(8,128)(2,1)} %copy-done.3) | copy-start | bytes 4718596
  144.4 59.5 %copy-start.6 = (bf16[880,128]{1,0:T(8,128)(2,1)}, bf16[880,128]{1,0:T(8,128)(2,1)S(1)}, u32[]{:S(2)}) copy-start(bf16[880,128]{1,0:T(8,128)(2,1)S(1)} %collective-permute-done.4) | copy-start | bytes 675844
  144.5 59.5 %copy-start.9 = (bf16[880,128]{1,0:T(8,128)(2,1)}, bf16[880,128]{1,0:T(8,128)(2,1)S(1)}, u32[]{:S(2)}) copy-start(bf16[880,128]{1,0:T(8,128)(2,1)S(1)} %collective-permute-done.3) | copy-start | bytes 675844
  144.5 59.5 %copy-start.12 = (bf16[880,128]{1,0:T(8,128)(2,1)}, bf16[880,128]{1,0:T(8,128)(2,1)S(1)}, u32[]{:S(2)}) copy-start(bf16[880,128]{1,0:T(8,128)(2,1)S(1)} %collective-permute-done.2) | copy-start | bytes 675844
  144.5 26.7 %collective-permute-start.5 = (f16[1040,256]{1,0:T(8,128)(2,1)S(1)}, f16[1040,256]{1,0:T(8,128)(2,1)S(1)}, u32[]{:S(2)}, u32[]{:S(2)}) collective-permute-start(f16[1040,256]{1,0:T(8,128)(2,1)S(1)} %get-tuple-element.95), channel_id=1, source_target_pairs={{0,32},{32,64},{64,96},{96,0},{1,33},{33,65},{65,97},{97,1},{2,34}... | collective-permute-start | bytes 1597448 | tf_op jit(solution)/shard_map/ppermute | solution.py:326
  147.8 23.4 %collective-permute-start.6 = (f16[1040,256]{1,0:T(8,128)(2,1)S(1)}, f16[1040,256]{1,0:T(8,128)(2,1)S(1)}, u32[]{:S(2)}, u32[]{:S(2)}) collective-permute-start(f16[1040,256]{1,0:T(8,128)(2,1)S(1)} %get-tuple-element.96), channel_id=1, source_target_pairs={{0,64},{32,96},{64,0},{96,32},{1,65},{33,97},{65,1},{97,33},{2,66}... | collective-permute-start | bytes 1597448 | tf_op jit(solution)/shard_map/ppermute | solution.py:326
  147.9 26.9 %collective-permute-start.7 = (f16[1040,256]{1,0:T(8,128)(2,1)S(1)}, f16[1040,256]{1,0:T(8,128)(2,1)S(1)}, u32[]{:S(2)}, u32[]{:S(2)}) collective-permute-start(f16[1040,256]{1,0:T(8,128)(2,1)S(1)} %get-tuple-element.97), channel_id=1, source_target_pairs={{0,96},{32,0},{64,32},{96,64},{1,97},{33,1},{65,33},{97,65},{2,98}... | collective-permute-start | bytes 1597448 | tf_op jit(solution)/shard_map/ppermute | solution.py:326
  175.6 7.8 %collective-permute-start.8 = (f32[4,1552,128]{2,1,0:T(8,128)}, f32[4,1552,128]{2,1,0:T(8,128)}, u32[]{:S(2)}, u32[]{:S(2)}) collective-permute-start(f32[4,1552,128]{2,1,0:T(8,128)} %get-tuple-element.103), channel_id=1, source_target_pairs={{0,16},{16,0},{1,17},{17,1},{2,18},{18,2},{3,19},{19,3},{4,20},{20... | collective-permute-start | bytes 9535496 | tf_op jit(solution)/shard_map/ppermute | solution.py:303
  177.3 4.0 %collective-permute-start.9 = (f32[8,128]{1,0:T(8,128)S(1)}, f32[8,128]{1,0:T(8,128)S(1)}, u32[]{:S(2)}, u32[]{:S(2)}) collective-permute-start(f32[8,128]{1,0:T(8,128)S(1)} %get-tuple-element.104), channel_id=1, source_target_pairs={{0,16},{16,0},{1,17},{17,1},{2,18},{18,2},{3,19},{19,3},{4,20},{20... | collective-permute-start | bytes 12296 | tf_op jit(solution)/shard_map/ppermute | solution.py:304
  183.4 12.1 %copy-start.20 = (f16[1040,256]{1,0:T(8,128)(2,1)S(1)}, f16[1040,256]{1,0:T(8,128)(2,1)}, u32[]{:S(2)}) copy-start(f16[1040,256]{1,0:T(8,128)(2,1)} %copy-done.19) | copy-start | bytes 1597444
  188.2 7.3 %collective-permute-start.11 = (f32[8,128]{1,0:T(8,128)S(1)}, f32[8,128]{1,0:T(8,128)S(1)}, u32[]{:S(2)}, u32[]{:S(2)}) collective-permute-start(f32[8,128]{1,0:T(8,128)S(1)} %broadcast_in_dim.38), channel_id=1, source_target_pairs={{0,32},{32,64},{64,96},{96,0},{1,33},{33,65},{65,97},{97,1},{2,34}... | collective-permute-start | bytes 12296 | tf_op jit(solution)/shard_map/ppermute | solution.py:330
  189.2 14.6 %collective-permute-start.12 = (f32[8,128]{1,0:T(8,128)S(1)}, f32[8,128]{1,0:T(8,128)S(1)}, u32[]{:S(2)}, u32[]{:S(2)}) collective-permute-start(f32[8,128]{1,0:T(8,128)S(1)} %broadcast_in_dim.38), channel_id=1, source_target_pairs={{0,96},{32,0},{64,32},{96,64},{1,97},{33,1},{65,33},{97,65},{2,98}... | collective-permute-start | bytes 12296 | tf_op jit(solution)/shard_map/ppermute | solution.py:330
  190.3 13.5 %collective-permute-start.10 = (f32[8,128]{1,0:T(8,128)S(1)}, f32[8,128]{1,0:T(8,128)S(1)}, u32[]{:S(2)}, u32[]{:S(2)}) collective-permute-start(f32[8,128]{1,0:T(8,128)S(1)} %broadcast_in_dim.38), channel_id=1, source_target_pairs={{0,64},{32,96},{64,0},{96,32},{1,65},{33,97},{65,1},{97,33},{2,66}... | collective-permute-start | bytes 12296 | tf_op jit(solution)/shard_map/ppermute | solution.py:330
  190.9 19.3 %collective-permute-start.14 = (f16[1552,128]{1,0:T(8,128)(2,1)}, f16[1552,128]{1,0:T(8,128)(2,1)}, u32[]{:S(2)}, u32[]{:S(2)}) collective-permute-start(f16[1552,128]{1,0:T(8,128)(2,1)} %get-tuple-element.117), channel_id=1, source_target_pairs={{0,32},{32,64},{64,96},{96,0},{1,33},{33,65},{65,97},{97,1},{2,34}... | collective-permute-start | bytes 1191944 | tf_op jit(solution)/shard_map/ppermute | solution.py:326
  193.1 17.1 %collective-permute-start.15 = (f16[1552,128]{1,0:T(8,128)(2,1)}, f16[1552,128]{1,0:T(8,128)(2,1)}, u32[]{:S(2)}, u32[]{:S(2)}) collective-permute-start(f16[1552,128]{1,0:T(8,128)(2,1)} %get-tuple-element.118), channel_id=1, source_target_pairs={{0,64},{32,96},{64,0},{96,32},{1,65},{33,97},{65,1},{97,33},{2,66}... | collective-permute-start | bytes 1191944 | tf_op jit(solution)/shard_map/ppermute | solution.py:326
  195.5 18.4 %collective-permute-start.16 = (f16[1552,128]{1,0:T(8,128)(2,1)}, f16[1552,128]{1,0:T(8,128)(2,1)}, u32[]{:S(2)}, u32[]{:S(2)}) collective-permute-start(f16[1552,128]{1,0:T(8,128)(2,1)} %get-tuple-element.119), channel_id=1, source_target_pairs={{0,96},{32,0},{64,32},{96,64},{1,97},{33,1},{65,33},{97,65},{2,98}... | collective-permute-start | bytes 1191944 | tf_op jit(solution)/shard_map/ppermute | solution.py:326
  196.9 25.2 %all-to-all-start.2 = ((f32[16,64,256]{2,1,0:T(8,128)}), f32[16,64,256]{2,1,0:T(8,128)S(1)}, u32[]{:S(2)}, u32[]{:S(2)}) async-start(f32[16,64,256]{2,1,0:T(8,128)} %bitcast.24), calls=%async_computation.2 | async-start | bytes 2097152 | tf_op jit(solution)/shard_map/all_to_all | solution.py:517
  203.8 1.2 collective-permute-start.13
  204.1 14.4 %collective-permute-start.17 = (bf16[4,880,128]{2,1,0:T(8,128)(2,1)S(1)}, bf16[4,880,128]{2,1,0:T(8,128)(2,1)S(1)}, u32[]{:S(2)}, u32[]{:S(2)}) collective-permute-start(bf16[4,880,128]{2,1,0:T(8,128)(2,1)S(1)} %pad_maximum_fusion.1), channel_id=1, source_target_pairs={{0,16},{16,0},{1,17},{17,1},{2,18},{18,2},{3,19},{19,3},{4,20},{20... | collective-permute-start | bytes 2703368 | tf_op jit(solution)/shard_map/ppermute | solution.py:431
  222.1 24.7 %all-to-all-start.3 = ((f32[16,128,128]{2,1,0:T(8,128)}), f32[16,128,128]{2,1,0:T(8,128)S(1)}, u32[]{:S(2)}, u32[]{:S(2)}) async-start(f32[16,128,128]{2,1,0:T(8,128)} %pad_maximum_fusion), calls=%async_computation.3 | async-start | bytes 2097152 | tf_op jit(solution)/shard_map/all_to_all | solution.py:533
  (15 other events, 37.6 us)

commit v2 on v1

v2 whole, which is shorter than its diff:
```python
import functools
import math

import jax
import jax.numpy as jnp
import numpy as np
from jax import lax
from jax.experimental import pallas as pl
from jax.experimental.pallas import tpu as pltpu
from jax.sharding import Mesh
from jax.sharding import PartitionSpec as P

BLOCK = 128
PLANE = ("z", "y")
EXPERTS = 16
TOK = 256
CAP = 64
MIB = 1024 * 1024
UP = [(i, (i + 1) % 4) for i in range(4)]
DOWN = [(i, (i - 1) % 4) for i in range(4)]
OPPOSITE = [(i, (i + 2) % 4) for i in range(4)]
SWAP = [(0, 1), (1, 0)]
bf16, f16, f32, i32 = jnp.bfloat16, jnp.float16, jnp.float32, jnp.int32
SLAB_ROWS, ROUTE_ROWS = 4 * TOK, 16
FIRST_ROWS = SLAB_ROWS + ROUTE_ROWS + 2 * TOK
SECOND_ROWS = TOK + TOK // 2
EXTRA = 16


def sine_coefficients():
    nodes = 0.5 * np.cos(np.pi * (np.arange(400) + 0.5) / 800)
    powers = np.stack([nodes ** (2 * k + 1) for k in range(8)], 1)
    scale = 1.0 / np.abs(powers).max(0)
    fit = np.linalg.lstsq(powers * scale, np.sin(2 * np.pi * nodes), rcond=None)[0]
    return [float(c) for c in fit * scale]


SINE = sine_coefficients()


def sine_turns(turns):
    r = turns - jnp.round(turns)
    s = r * r
    total = jnp.full_like(r, SINE[-1])
    for c in SINE[-2::-1]:
        total = total * s + c
    return total * r


def build_kernel(tokens_ref, routes_ref, first_ref, second_ref, slab):
    i = pl.program_id(0)

    @pl.when(i == 0)
    def _():
        for tile in range(4):
            turned = tokens_ref[:, tile * 128 : (tile + 1) * 128].astype(f32).T.astype(bf16)
            slab[tile * 128 : (tile + 1) * 128, :] = turned[:, :128]
            slab[512 + tile * 128 : 512 + (tile + 1) * 128, :] = turned[:, 128:]

    def tile(k):
        return tokens_ref[:, pl.ds(pl.multiple_of(k * 128, 128), 128)]

    low = lax.broadcasted_iota(i32, (128, 128), 1) < 64
    last = tile(3 * EXPERTS + i).astype(f32)
    turned = pltpu.roll(last, 64, 1)
    for half, (left, right) in enumerate(((last, turned), (turned, last))):
        to = 2 * i + half
        first_ref[half, :SLAB_ROWS, :] = slab[...]
        first_ref[half, SLAB_ROWS : SLAB_ROWS + ROUTE_ROWS, :] = routes_ref[...]
        start = SLAB_ROWS + ROUTE_ROWS
        first_ref[half, start : start + TOK, :] = tile(to)
        first_ref[half, start + TOK : start + 2 * TOK, :] = tile(EXPERTS + to)
        second_ref[half, :TOK, :] = tile(2 * EXPERTS + to)
        second_ref[half, TOK:, :] = jnp.where(low, left[:128], right[128:]).astype(bf16)


def build(tokens, routes_rows):
    return pl.pallas_call(
        build_kernel,
        grid=(EXPERTS // 2,),
        in_specs=[
            pl.BlockSpec((TOK, tokens.shape[1]), lambda i: (0, 0)),
            pl.BlockSpec((ROUTE_ROWS, 128), lambda i: (0, 0)),
        ],
        out_specs=[
            pl.BlockSpec((2, FIRST_ROWS, 128), lambda i: (i, 0, 0)),
            pl.BlockSpec((2, SECOND_ROWS, 128), lambda i: (i, 0, 0)),
        ],
        out_shape=[
            pltpu.HBM((EXPERTS, FIRST_ROWS, 128), bf16),
            pltpu.HBM((EXPERTS, SECOND_ROWS, 128), bf16),
        ],
        scratch_shapes=[pltpu.VMEM((SLAB_ROWS, 128), bf16)],
        compiler_params=pltpu.CompilerParams(vmem_limit_bytes=24 * MIB),
        name="build",
    )(pltpu.with_memory_space_constraint(tokens, pltpu.HBM), routes_rows)


def places_of(routes_rows):
    rows = routes_rows.astype(f32)
    one = jnp.concatenate([rows[0:1], rows[1:2]], axis=1)
    two = jnp.concatenate([rows[2:3], rows[3:4]], axis=1)
    expert = lax.broadcasted_iota(i32, (EXPERTS, TOK), 0).astype(f32)
    member = jnp.where((one == expert) | (two == expert), 1.0, 0.0)
    before = lax.broadcasted_iota(i32, (TOK, TOK), 0) < lax.broadcasted_iota(i32, (TOK, TOK), 1)
    earlier = jnp.dot(
        member.astype(bf16), jnp.where(before, 1.0, 0.0).astype(bf16), preferred_element_type=f32
    )
    return jnp.where(member > 0, earlier, -1.0)


def fill_pick(places, pick_ref, flip):
    slot = lax.broadcasted_iota(i32, (CAP, TOK), 0).astype(f32)
    for e in range(EXPERTS):
        hit = jnp.broadcast_to(places[e : e + 1, :], (CAP, TOK)) == slot
        to = (e ^ flip) * CAP
        pick_ref[to : to + CAP, :] = jnp.where(hit, 1.0, 0.0).astype(bf16)


def split_rows(here_ref, part_ref, keep_ref, send_ref, store):
    x, core = here_ref[0], here_ref[1]
    for step in range(4):
        owner = lax.rem(x + step, 4) * 2
        store(keep_ref, step, part_ref[owner + core])
        store(send_ref, step, part_ref[owner + 1 - core])


def note_largest(top_ref, product):
    largest = jnp.max(jnp.abs(product).reshape(-1, 8, product.shape[1]), axis=0)
    top_ref[...] = jnp.maximum(top_ref[...], jnp.maximum(largest[:, :128], largest[:, 128:]))


def slab_in_slots(pair, blocks, picks, slab):
    low = lax.broadcasted_iota(i32, (512, 128), 1) < CAP
    lanes = pl.ds(pl.multiple_of(pair * 128, 128), 128)
    rows = [jnp.concatenate([block[:512, :], block[512:SLAB_ROWS, :]], axis=1) for block in blocks]
    for quarter in range(4):
        got = [
            lax.dot_general(
                rows[source],
                picks[source][quarter * 256 : (quarter + 1) * 256, :],
                (((1,), (1,)), ((), ())),
                preferred_element_type=f32,
            ).astype(bf16)
            for source in range(2)
        ]
        for half in range(2):
            m = 2 * quarter + half
            a, b = (g[:, half * 128 : (half + 1) * 128] for g in got)
            slab[2 * m, :, lanes] = jnp.where(low, a, b)
            slab[2 * m + 1, :, lanes] = jnp.where(low, b, a)


def columns_in_slots(pair, cols, picks, held):
    for quarter in range(4):
        got = [
            jnp.dot(
                picks[source][quarter * 256 : (quarter + 1) * 256, :],
                cols[source],
                preferred_element_type=f32,
            ).astype(bf16)
            for source in range(2)
        ]
        for source in range(2):
            for block in range(4):
                e = (4 * quarter + block) ^ source
                offset = CAP * ((e + source) % 2)
                held[e, pl.ds(pl.multiple_of(pair * 128 + offset, CAP), CAP), :] = got[source][
                    block * CAP : (block + 1) * CAP
                ]


def slab_copy(slab, out_ref, sems, pair):
    lanes = pl.ds(pl.multiple_of(pair * 128, 128), 128)
    return pltpu.make_async_copy(slab.at[:, :, lanes], out_ref.at[pair], sems.at[pair])


def finish_notes(top_ref, counts):
    largest = jnp.broadcast_to(jnp.max(top_ref[...], keepdims=True), top_ref.shape)
    top_ref[...] = jnp.where(lax.broadcasted_iota(i32, top_ref.shape, 0) == 0, largest, counts)


def count_tokens(routes_rows):
    rows = routes_rows.astype(f32)
    expert = lax.broadcasted_iota(i32, (128, 128), 0).astype(f32)
    named = sum(jnp.where(rows[k : k + 1] == expert, 1.0, 0.0) for k in range(4))
    return lax.dot_general(
        jnp.ones((8, 128), bf16),
        named.astype(bf16),
        (((1,), (1,)), ((), ())),
        preferred_element_type=f32,
    )


def product0_kernel(
    here_ref, in_ref, keep_ref, send_ref, top_ref, slab_ref, places_ref, pick0, pick1, held, slab, sems, part, counts
):
    step = pl.program_id(0)

    @pl.when(step == 0)
    def _():
        top_ref[...] = jnp.zeros_like(top_ref)
        counts[...] = jnp.zeros_like(counts)

    @pl.when(step < 8)
    def _():
        blocks = [in_ref.at[source] for source in range(2)]
        start = SLAB_ROWS + ROUTE_ROWS
        cols = [
            jnp.concatenate(
                [block[start : start + TOK, :], block[start + TOK : start + 2 * TOK, :]], axis=1
            )
            for block in blocks
        ]
        picks = (pick0, pick1)
        for source in range(2):
            routes_rows = blocks[source][SLAB_ROWS : SLAB_ROWS + ROUTE_ROWS, :]
            counts[...] += count_tokens(routes_rows)
            places = places_of(routes_rows)
            places_ref[source] = places
            fill_pick(places, picks[source], source)
        slab_in_slots(step, blocks, picks, slab)
        slab_copy(slab, slab_ref, sems, step).start()
        columns_in_slots(step, cols, picks, held)

    @pl.when(step >= 8)
    def _():
        products = [
            jnp.dot(slab[e], held[e], preferred_element_type=f32)
            for e in (2 * (step - 8), 2 * (step - 8) + 1)
        ]
        for k in range(2):
            note_largest(top_ref, products[k])
            for tile in range(2):
                rows = slice(tile * 64, (tile + 1) * 64)
                part[k, :, rows, :] = products[k][:, tile * 128 : (tile + 1) * 128].reshape(8, 64, 128)
        for k in range(2):

            def store(ref, at, value):
                ref[at, k * 128 : (k + 1) * 128] = value

            split_rows(here_ref, part.at[k], keep_ref, send_ref, store)

    @pl.when(step == 15)
    def _():
        finish_notes(top_ref, counts[...])
        for pair in range(8):
            slab_copy(slab, slab_ref, sems, pair).wait()


PICKS = [pltpu.VMEM((1024, TOK), bf16)] * 2
HELD = pltpu.VMEM((EXPERTS, 1024, 256), bf16)


def early(i, here):
    return (jnp.minimum(i, 7), 0, 0)


def product0(here, first):
    rows = pl.BlockSpec((4, 256, 128), lambda i, here: (0, jnp.maximum(i - 8, 0), 0))
    return pl.pallas_call(
        product0_kernel,
        grid_spec=pltpu.PrefetchScalarGridSpec(
            num_scalar_prefetch=1,
            grid=(16,),
            in_specs=[pl.BlockSpec((2, FIRST_ROWS, 128), early)],
            out_specs=[
                rows,
                rows,
                pl.BlockSpec((8, 128), lambda i, here: (0, 0)),
                pl.BlockSpec(memory_space=pl.ANY),
                pl.BlockSpec((2, EXPERTS, TOK), early),
            ],
            scratch_shapes=[
                *PICKS,
                HELD,
                pltpu.VMEM((EXPERTS, 512, 1024), bf16),
                pltpu.SemaphoreType.DMA((8,)),
                pltpu.VMEM((2, 8, 128, 128), f32),
                pltpu.VMEM((8, 128), f32),
            ],
        ),
        out_shape=[pltpu.HBM((4, EXPERTS * 128 + EXTRA, 128), f32)] * 2
        + [
            jax.ShapeDtypeStruct((8, 128), f32),
            pltpu.HBM((8, EXPERTS, 512, 128), bf16),
            jax.ShapeDtypeStruct((EXPERTS, EXPERTS, TOK), f32),
        ],
        compiler_params=pltpu.CompilerParams(vmem_limit_bytes=40 * MIB),
        cost_estimate=pl.CostEstimate(flops=11 * 10**9, bytes_accessed=16 * 10**6, transcendentals=0),
        name="product0",
    )(here, pltpu.with_memory_space_constraint(first, pltpu.HBM))


def product1_kernel(
    here_ref, places_ref, cols_ref, slab_ref, keep_ref, send_ref, top_ref, pick0, pick1, held, part, slab, sems
):
    step = pl.program_id(0)

    def fetch(pair):
        return pltpu.make_async_copy(
            slab_ref.at[:, pl.ds(2 * pair, 2)], slab.at[pair], sems.at[pair]
        )

    @pl.when(step == 0)
    def _():
        top_ref[...] = jnp.zeros_like(top_ref)
        for pair in range(8):
            fetch(pair).start()

    @pl.when(step < 8)
    def _():
        picks = (pick0, pick1)
        cols = []
        for source in range(2):
            fill_pick(places_ref[source], picks[source], source)
            last = cols_ref[source, TOK:, :]
            turned = pltpu.roll(last.astype(f32), 64, 1).astype(bf16)
            last = jnp.concatenate([last, turned], axis=0)
            cols.append(jnp.concatenate([cols_ref[source, :TOK, :], last], axis=1))
        columns_in_slots(step, cols, picks, held)

    @pl.when(step >= 8)
    def _():
        fetch(step - 8).wait()
        products = [
            jnp.dot(
                jnp.concatenate([slab[step - 8, pair, k] for pair in range(8)], axis=1),
                held[2 * (step - 8) + k],
                preferred_element_type=f32,
            )
            for k in range(2)
        ]
        low = lax.broadcasted_iota(i32, (8, 32, 128), 2) < 64
        for k in range(2):
            note_largest(top_ref, products[k])
            part[k, :, :64, :] = products[k][:, :128].reshape(8, 64, 128)
            halves = products[k][:, 128:].reshape(8, 2, 32, 128)
            turned = pltpu.roll(products[k][:, 128:], 64, 1).reshape(8, 2, 32, 128)
            part[k, :, 64:, :] = jnp.where(low, halves[:, 0], turned[:, 1])
        for k in range(2):

            def store(ref, at, value):
                ref[at, k * 96 : (k + 1) * 96] = value

            split_rows(here_ref, part.at[k], keep_ref, send_ref, store)

    @pl.when(step == 15)
    def _():
        finish_notes(top_ref, 0.0)


def product1(here, places, second, slab):
    rows = pl.BlockSpec((4, 192, 128), lambda i, here: (0, jnp.maximum(i - 8, 0), 0))
    return pl.pallas_call(
        product1_kernel,
        grid_spec=pltpu.PrefetchScalarGridSpec(
            num_scalar_prefetch=1,
            grid=(16,),
            in_specs=[
                pl.BlockSpec((2, EXPERTS, TOK), early),
                pl.BlockSpec((2, SECOND_ROWS, 128), early),
                pl.BlockSpec(memory_space=pl.ANY),
            ],
            out_specs=[rows, rows, pl.BlockSpec((8, 128), lambda i, here: (0, 0))],
            scratch_shapes=[
                *PICKS,
                HELD,
                pltpu.VMEM((2, 8, 96, 128), f32),
                pltpu.VMEM((8, 8, 2, 512, 128), bf16),
                pltpu.SemaphoreType.DMA((8,)),
            ],
        ),
        out_shape=[pltpu.HBM((4, EXPERTS * 96 + EXTRA, 128), f32)] * 2
        + [jax.ShapeDtypeStruct((8, 128), f32)],
        compiler_params=pltpu.CompilerParams(vmem_limit_bytes=40 * MIB),
        cost_estimate=pl.CostEstimate(flops=11 * 10**9, bytes_accessed=16 * 10**6, transcendentals=0),
        name="product1",
    )(here, places, second, slab)


def over_core(send, top):
    return lax.ppermute(send, "core", SWAP), top + lax.ppermute(top, "core", SWAP)


def sum_over_core(keep, other, top):
    top, counts = top[:1], top[1:2]
    exponent = jnp.clip(jnp.floor(jnp.log2(32000.0 / jnp.maximum(top, 1e-30))), -100.0, 100.0)
    exponent, factor = lax.optimization_barrier((exponent, jnp.exp2(exponent)))
    rows = keep.shape[1] - EXTRA
    row = lax.broadcasted_iota(i32, keep.shape[1:], 0)
    more = jnp.where(row == rows + 1, counts, exponent)
    others = [
        jnp.where(row < rows, (keep[i] + other[i]) * factor, more).astype(f16) for i in (1, 2, 3)
    ]
    return (keep[0], other[0], exponent, counts), others


def sum_over_x(own, others):
    rows = own[0].shape[0] - EXTRA
    exponents = [value[rows : rows + 1].astype(f32) for value in others]
    one, two, three = (
        value.astype(f32) * jnp.exp2(-exponent) for value, exponent in zip(others, exponents)
    )
    least = functools.reduce(jnp.minimum, exponents, own[2]) - 2.0
    total = (own[0] + own[1] + two) + (one + three)
    counts = own[3] + sum(value[rows + 1 : rows + 2].astype(f32) for value in others)
    return (total * jnp.exp2(least))[:rows].astype(f16), least, counts


def over_x(others):
    return [lax.ppermute(value, "x", pairs) for value, pairs in zip(others, (UP, OPPOSITE, DOWN))]


def order_kernel(scale_ref, a_ref, b_ref, out_ref):
    scale = scale_ref[0]
    for i in range(EXPERTS):
        out_ref[:, i * 128 : (i + 1) * 128] = a_ref[i, :64, :] * scale
        out_ref[:, (16 + i) * 128 : (17 + i) * 128] = a_ref[i, 64:, :] * scale
        out_ref[:, (32 + i) * 128 : (33 + i) * 128] = b_ref[i, :64, :] * scale
    low = lax.broadcasted_iota(i32, (32, 128), 1) < 64
    for t in range(8):
        left, right = b_ref[2 * t, 64:, :], b_ref[2 * t + 1, 64:, :]
        columns = slice((48 + t) * 128, (49 + t) * 128)
        out_ref[:32, columns] = jnp.where(low, left, pltpu.roll(right, 64, 1)) * scale
        out_ref[32:, columns] = jnp.where(low, pltpu.roll(left, 64, 1), right) * scale


def put_in_order(scale, a, b):
    smem, vmem = pl.BlockSpec(memory_space=pltpu.SMEM), pl.BlockSpec(memory_space=pltpu.VMEM)
    return pl.pallas_call(
        order_kernel,
        in_specs=[smem, vmem, vmem],
        out_specs=vmem,
        out_shape=jax.ShapeDtypeStruct((64, 7168), f32),
        compiler_params=pltpu.CompilerParams(vmem_limit_bytes=16 * MIB),
        name="put_in_order",
    )(scale, a, b)


def columns_kernel(block_ref, levels_ref, pivots_ref, upper_ref, turned_ref, snapped_ref, errors_ref, now, out, err):
    block = block_ref[...].astype(f32).T
    now[...] = block
    largest = jnp.max(jnp.abs(block), axis=0, keepdims=True)
    spacing = (largest + 1e-05) / levels_ref[...].astype(f32)
    per_turn = 1.0 / spacing
    reach = 0.9 * spacing / (2.0 * math.pi)
    lane = lax.broadcasted_iota(i32, (8, BLOCK), 1)

    def group(b, carry):
        at = pl.multiple_of(b * 8, 8)
        tile = now[pl.ds(at, 8), :]
        turned = turned_ref[pl.ds(at, 8), :]
        near = [
            jnp.sum(jnp.where(lane == at + i, turned, 0.0), axis=1, keepdims=True) for i in range(8)
        ]
        snapped, errors = [], []
        for i in range(8):
            values = tile[i : i + 1, :]
            moved = values - reach * sine_turns(values * per_turn)
            error = (values - moved) * pivots_ref[at + i]
            tile = tile - near[i] * error
            snapped.append(moved)
            errors.append(error)
        errors = jnp.concatenate(errors, axis=0)
        out[pl.ds(at, 8), :] = jnp.concatenate(snapped, axis=0)
        err[pl.ds(at, 8), :] = errors
        now[...] -= lax.dot_general(
            upper_ref[pl.ds(at, 8), :],
            errors,
            (((0,), (0,)), ((), ())),
            precision=lax.Precision.HIGHEST,
            preferred_element_type=f32,
        )
        return carry

    lax.fori_loop(0, BLOCK // 8, group, 0)
    snapped_ref[...] = out[...].T
    errors_ref[...] = err[...].T


def block_update(rows, levels, pivots, upper):
    whole = lambda *shape: pl.BlockSpec(shape, lambda i: (0,) * len(shape))
    count = rows.shape[0]
    return pl.pallas_call(
        columns_kernel,
        grid=(1,),
        in_specs=[
            whole(count, BLOCK),
            whole(1, count),
            pl.BlockSpec(memory_space=pltpu.SMEM),
            whole(BLOCK, BLOCK),
            whole(BLOCK, BLOCK),
        ],
        out_specs=[whole(count, BLOCK)] * 2,
        out_shape=[jax.ShapeDtypeStruct((count, BLOCK), f32)] * 2,
        scratch_shapes=[pltpu.VMEM((BLOCK, count), f32)] * 3,
        compiler_params=pltpu.CompilerParams(vmem_limit_bytes=16 * MIB),
        cost_estimate=pl.CostEstimate(flops=10**9, bytes_accessed=2 * 10**6, transcendentals=0),
        name="block_update",
    )(pltpu.with_memory_space_constraint(rows, pltpu.HBM), levels, 1.0 / pivots, upper, upper.T)


def ahead_over_x(mine):
    return [mine] + [lax.ppermute(mine, "x", pairs) for pairs in (DOWN, OPPOSITE, UP)]


def later_kernel(here_ref, errors_ref, own_ref, other_ref, *refs):
    *weight_refs, out_ref, panel, parts = refs
    i = pl.program_id(0)
    wide = panel.shape[0] // 8
    count = errors_ref.shape[0]

    @pl.when(i == 0)
    def _():
        x, core = here_ref[0], here_ref[1]
        for at in range(4):
            ahead = lax.rem(at + 4 - x, 4)
            mine = pl.multiple_of((2 * at + core) * wide, 16)
            theirs = pl.multiple_of((2 * at + 1 - core) * wide, 16)
            panel[pl.ds(mine, wide), :] = own_ref[ahead, :wide, :]
            panel[pl.ds(theirs, wide), :] = other_ref[ahead, :wide, :]
        errors = errors_ref[...]
        for k in range(3):
            part = errors.astype(bf16)
            errors = errors - part.astype(f32)
            parts[k * count : (k + 1) * count, :] = part

    got = lax.dot_general(
        parts[...],
        panel[pl.ds(pl.multiple_of(i * 640, 128), 640), :],
        (((1,), (1,)), ((), ())),
        preferred_element_type=f32,
    )
    total = (got[:count] + got[count : 2 * count]) + got[2 * count :]
    for k, ref in enumerate(weight_refs):
        out_ref[:, k * 128 : (k + 1) * 128] = ref[...].astype(f32) - total[:, k * 128 : (k + 1) * 128]


def later_columns(here, rows, errors, own, other):
    count, later = rows.shape[0], rows.shape[1] - BLOCK
    columns = [
        pl.BlockSpec((count, 128), functools.partial(lambda k, i, here: (0, 5 * i + k), k))
        for k in range(1, 6)
    ]
    whole = lambda a: pl.BlockSpec(a.shape, lambda i, here: (0,) * a.ndim)
    return pl.pallas_call(
        later_kernel,
        grid_spec=pltpu.PrefetchScalarGridSpec(
            num_scalar_prefetch=1,
            grid=(later // 640,),
            in_specs=[whole(errors), whole(own), whole(other)] + columns,
            out_specs=pl.BlockSpec((count, 640), lambda i, here: (0, i)),
            scratch_shapes=[pltpu.VMEM((later, BLOCK), bf16), pltpu.VMEM((3 * count, BLOCK), bf16)],
        ),
        out_shape=pltpu.HBM((count, later), f32),
        compiler_params=pltpu.CompilerParams(vmem_limit_bytes=24 * MIB),
        cost_estimate=pl.CostEstimate(flops=15 * 10**8, bytes_accessed=13 * 10**6, transcendentals=0),
        name="later_columns",
    )(here, errors, own, other, *[pltpu.with_memory_space_constraint(rows, pltpu.HBM)] * 5)


def on_device(tokens, routes, weight, levels, pivots, panel_diag, panel_rest):
    x, core = lax.axis_index("x"), lax.axis_index("core")
    place = lax.axis_index("z") * 4 + lax.axis_index("y")
    routes_rows = jnp.pad(routes.T.reshape(4, 128).astype(bf16), ((0, ROUTE_ROWS - 4), (0, 0)))
    exchange = functools.partial(
        lax.all_to_all, axis_name=PLANE, split_axis=0, concat_axis=0, tiled=True
    )
    here = jnp.stack([x, core]).astype(i32)

    first, second = build(tokens, routes_rows)
    first, here, place, pivots = lax.optimization_barrier((first, here, place, pivots))
    first = exchange(first)
    first, second, weight, levels, panel_diag, panel_rest, pivots = lax.optimization_barrier(
        (first, second, weight, levels, panel_diag, panel_rest, pivots)
    )
    second = exchange(second)
    keep, send, top, slab, places = product0(here, first)
    keep, send, top, second, slab, places, panel_rest = lax.optimization_barrier(
        (keep, send, top, second, slab, places, panel_rest)
    )
    panel = ahead_over_x(panel_rest[0].T.astype(bf16))
    own, others = sum_over_core(keep, *over_core(send, top))
    places, second, slab, others = lax.optimization_barrier((places, second, slab, others))
    others = over_x(others)
    keep, send, top = product1(here, places, second, slab)
    keep, send, top, others, panel, weight = lax.optimization_barrier(
        (keep, send, top, others, panel, weight)
    )
    total, least, counts = sum_over_x(own, others)
    panel = jnp.stack(panel)
    own, others = sum_over_core(keep, *over_core(send, top))

    others, rows, panel_diag, panel = lax.optimization_barrier((others, weight[0], panel_diag, panel))
    others = over_x(others)
    upper = jnp.triu(panel_diag[0], 1)
    snapped, errors = block_update(rows, levels, pivots[0], upper)
    other_panel = lax.ppermute(panel, "core", SWAP)
    others, errors, other_panel, total, least = lax.optimization_barrier(
        (others, errors, other_panel, total, least)
    )
    tail, last, _ = sum_over_x(own, others)
    sent = [total.reshape(EXPERTS, 128, 128), tail.reshape(EXPERTS, 96, 128)]
    first_rows = lax.broadcasted_iota(i32, (EXPERTS, 16, 128), 1) < 8
    sent.append(jnp.where(first_rows, least, last).astype(f16))
    sums = exchange(jnp.concatenate(sent, axis=1))

    remainder = later_columns(here, rows, errors, panel, other_panel)

    own_count = lax.dynamic_index_in_dim(counts[0], place, 0, keepdims=True)
    total = sums[:, :128].astype(f32) * jnp.exp2(-sums[:, 224:225].astype(f32))
    tail = sums[:, 128:224].astype(f32) * jnp.exp2(-sums[:, 232:233].astype(f32))
    hessian = put_in_order(2.0 / own_count, total, tail)
    return hessian[None], snapped[None], remainder[None]


def solution(mesh):
    devices = mesh.devices
    fine = Mesh(devices.reshape(4, 2, 4, 4), ("x", "core", "z", "y"))
    dp, every = ("x", "core"), ("x", "core", "z", "y")
    return jax.shard_map(
        on_device,
        mesh=fine,
        in_specs=(
            P(every, None),
            P(every, None),
            P(PLANE, dp, None),
            P(PLANE, dp),
            P(PLANE, None),
            P(PLANE, None, None),
            P(PLANE, None, dp),
        ),
        out_specs=(P(PLANE, dp, None),) * 3,
        check_vma=False,
    )
```

time: 251 us -> 217 us (0.86)
  other arithmetic: 27.7 us -> 13 us
  waiting for transfers between devices: 18.8 us -> 31.6 us
  starting transfers between devices: 33.8 us -> 21.9 us
  local copies, waits for them, and re-layouts: 9.24 us -> 0.62 us
  Pallas kernels: 73.3 us -> 65.4 us
  between operations: 3.91 us -> 0.85 us
    pallas_call x1, Pallas kernels: 20.7 us -> 13.2 us  [product1(): pl.pallas_call(product1_kernel, grid_spec=pltpu.PrefetchScalarGridSpec(nu...]
    all_to_all x2 -> x1, starting transfers between devices: 13.9 us -> 6.67 us  [on_device(): sums = exchange(jnp.concatenate(sent, axis=1))]
    unnamed x8 -> x0, other arithmetic: 7.18 us -> none
    unnamed x53 -> x12, local copies, waits for them, and re-layouts: 7.2 us -> 0.43 us
    ppermute x6, waiting for transfers between devices: 12.9 us -> 19.2 us  [over_x(): lax.ppermute(value, 'x', pairs)]
    ppermute x12 -> x8, waiting for transfers between devices: 2.59 us -> 6.68 us  [the longest x2 4.74 us: over_core(): lax.ppermute(top, 'core', SWAP)]
    pallas_call x3, Pallas kernels: 23.4 us -> 20.2 us  [the longest x1 11.2 us: later_columns(): pl.pallas_call(later_kernel, grid_spec=pltpu.PrefetchScalarGridSpec(num_s...]
    ppermute x6, starting transfers between devices: 9.28 us -> 6.22 us  [over_x(): lax.ppermute(value, 'x', pairs)]
  transfers between devices with their start and end apart: 21 -> 16, of which waited for: 8 -> 11; matrix products, arithmetic and copies ran while one was open for 9% -> 4% of each run, Pallas kernels for 24% -> 26%
where the time goes in v2:
time: 217 us; the launch traced here: 216 us
  blocking collectives  82.2 us (38%)
  Pallas kernels  65.4 us (30%)
  waiting for transfers between devices  31.6 us (15%)
  starting transfers between devices  21.9 us (10%)
  other arithmetic  13 us (6%)
    all_to_all x1, blocking collectives, on_device(): first = exchange(first)  82.2 us
    pallas_call x1, Pallas kernels, product0(): pl.pallas_call(product0_kernel, grid_spec=pltpu.PrefetchScalarGridSpec(nu...  21.9 us
    ppermute x6, waiting for transfers between devices, over_x(): lax.ppermute(value, 'x', pairs)  19.2 us
    pallas_call x1, Pallas kernels, product1(): pl.pallas_call(product1_kernel, grid_spec=pltpu.PrefetchScalarGridSpec(nu...  13.2 us
    pallas_call x1, Pallas kernels, later_columns(): pl.pallas_call(later_kernel, grid_spec=pltpu.PrefetchScalarGridSpec(num_s...  11.2 us
    pallas_call x1, Pallas kernels, block_update(): pl.pallas_call(columns_kernel, grid=(1,), in_specs=[whole(count, BLOCK),...  10.1 us
    pallas_call x1, Pallas kernels, build(): pl.pallas_call(build_kernel, grid=(EXPERTS // 2,), in_specs=[pl.BlockSpec...  6.79 us
    all_to_all x1, starting transfers between devices, on_device(): sums = exchange(jnp.concatenate(sent, axis=1))  6.67 us
  transfers between devices with their start and end apart: 16, of which 11 were waited for; matrix products, arithmetic and copies ran while one was open for 4% of the time, Pallas kernels for 26%

profile of v2, /device:TPU:6, one launch (start us, length us, event | category | flops | bytes accessed | tf_op | source)
XLA Modules:
  0.0 215.6 jit_solution(3210645444408735236)
XLA Ops:
  0.6 0.7 convert_bitcast_fusion.1
  1.4 6.8 %build.1 = (bf16[16,1552,128]{2,1,0:T(8,128)(2,1)}, bf16[16,384,128]{2,1,0:T(8,128)(2,1)}) custom-call(bf16[256,7168]{1,0:T(8,128)(2,1)} %tokens_ref.1, bf16[16,128]{1,0:T(8,128)(2,1)S(1)} %pad.4.routes_ref), custom_call_target="tpu_custom_call" | custom-call | tf_op jit(solution)/shard_map/build/pallas_call | solution.py:78
  8.2 82.2 %all_to_all.15.in_ref = bf16[16,1552,128]{2,1,0:T(8,128)(2,1)} all-to-all(bf16[16,1552,128]{2,1,0:T(8,128)(2,1)} %get-tuple-element.69), channel_id=1, replica_groups=mesh['x'=4,'core'=2,'z'=4,'y'=4] {'z','y'}, dimensions={0} | all-to-all | bytes 12713984 | tf_op jit(solution)/shard_map/all_to_all | solution.py:574
  90.4 3.7 %all-to-all-start.1 = ((bf16[16,384,128]{2,1,0:T(8,128)(2,1)}), bf16[16,384,128]{2,1,0:T(8,128)(2,1)S(1)}, u32[]{:S(2)}, u32[]{:S(2)}) async-start(bf16[16,384,128]{2,1,0:T(8,128)(2,1)} %get-tuple-element.76), calls=%async_computation.1 | async-start | bytes 3145728 | tf_op jit(solution)/shard_map/all_to_all | solution.py:578
  94.2 21.9 %product0.1 = (f32[4,2064,128]{2,1,0:T(8,128)}, f32[4,2064,128]{2,1,0:T(8,128)}, f32[8,128]{1,0:T(8,128)S(1)}, bf16[8,16,512,128]{3,2,1,0:T(8,128)(2,1)}, f32[16,16,256]{2,1,0:T(8,128)S(1)}) custom-call(s32[2]{0:T(128)S(1)} %pad_add_fusion.here_ref, bf16[16,1552,128]{2,1,0:T(8,128)(2,1)} %all_to_all.15.in_ref), custom_call_target="tpu_custom_call" | custom-call | flops 11000000512 | bytes 16000000 | tf_op jit(solution)/shard_map/product0/pallas_call | solution.py:261
  116.1 0.6 all-to-all-done.1.cols_ref
  117.2 0.9 collective-permute-start.5
  118.1 1.1 collective-permute-start.6
  119.2 2.1 collective-permute-start.7
  121.3 1.3 collective-permute-done
  122.6 1.5 collective-permute-done.1
  124.1 3.5 %fusion.2 = (f16[2064,128]{1,0:T(8,128)(2,1)S(1)}, f16[2064,128]{1,0:T(8,128)(2,1)S(1)}, f16[2064,128]{1,0:T(8,128)(2,1)S(1)}) fusion(f32[4,2064,128]{2,1,0:T(8,128)S(1)} %collective-permute-done.1, f32[4,2064,128]{2,1,0:T(8,128)} %get-tuple-element.84, f32[128]{0:T(128)S(1)} %bitcast.111, f32[128]{0:T(128)S(1)} %get-tuple-element.157, f32[128]{0:T(128)S(1)} %bitcast.114, ...), kind=kLoop, calls=%fused_computation.8 | loop fusion | flops 3434496 | bytes 7931424 | tf_op jit(solution)/shard_map/convert_element_type | solution.py:394
  127.6 0.5 collective-permute-start.2
  128.1 2.4 %collective-permute-start.3 = (f16[2064,128]{1,0:T(8,128)(2,1)S(1)}, f16[2064,128]{1,0:T(8,128)(2,1)S(1)}, u32[]{:S(2)}, u32[]{:S(2)}) collective-permute-start(f16[2064,128]{1,0:T(8,128)(2,1)S(1)} %get-tuple-element.95), channel_id=1, source_target_pairs={{0,64},{32,96},{64,0},{96,32},{1,65},{33,97},{65,1},{97,33},{2,66}... | collective-permute-start | bytes 1585160 | tf_op jit(solution)/shard_map/ppermute | solution.py:412
  130.8 13.2 %product1.1 = (f32[4,1552,128]{2,1,0:T(8,128)}, f32[4,1552,128]{2,1,0:T(8,128)}, f32[8,128]{1,0:T(8,128)S(1)}) custom-call(s32[2]{0:T(128)S(1)} %pad_add_fusion.here_ref, f32[16,16,256]{2,1,0:T(8,128)S(1)} %get-tuple-element.88.places_ref, bf16[16,384,128]{2,1,0:T(8,128)(2,1)S(1)} %all-to-all-done.1.cols_ref, ...), custom_call_target="tpu_custom_call" | custom-call | flops 11000000512 | bytes 16000000 | tf_op jit(solution)/shard_map/product1/pallas_call | solution.py:355
  144.6 10.2 %collective-permute-done.4 = f16[2064,128]{1,0:T(8,128)(2,1)S(1)} collective-permute-done((f16[2064,128]{1,0:T(8,128)(2,1)S(1)}, f16[2064,128]{1,0:T(8,128)(2,1)S(1)}, u32[]{:S(2)}, u32[]{:S(2)}) %collective-permute-start.4) | collective-permute-done | bytes 528416 | tf_op jit(solution)/shard_map/ppermute | solution.py:412
  154.8 1.5 fusion.3
  156.3 0.6 collective-permute-start.9
  157.0 3.5 %collective-permute-done.9 = f32[8,128]{1,0:T(8,128)S(1)} collective-permute-done((f32[8,128]{1,0:T(8,128)S(1)}, f32[8,128]{1,0:T(8,128)S(1)}, u32[]{:S(2)}, u32[]{:S(2)}) %collective-permute-start.9) | collective-permute-done | bytes 4128 | tf_op jit(solution)/shard_map/ppermute | solution.py:383
  160.7 2.6 %fusion.15 = (f16[1552,128]{1,0:T(8,128)(2,1)S(1)}, f16[1552,128]{1,0:T(8,128)(2,1)S(1)}, f16[1552,128]{1,0:T(8,128)(2,1)}) fusion(f32[4,1552,128]{2,1,0:T(8,128)S(1)} %collective-permute-done.8, f32[4,1552,128]{2,1,0:T(8,128)S(1)} %copy-done.1, f32[128]{0:T(128)S(1)} %bitcast.112, f32[128]{0:T(128)S(1)} %get-tuple-element.156, f32[128]{0:T(128)S(1)} %bitcast.116, ...), kind=kLoop, calls=%fused_computation.29 | loop fusion | flops 2582528 | bytes 5964320 | tf_op jit(solution)/shard_map/convert_element_type | solution.py:394
  164.4 2.1 collective-permute-start.10
  166.6 1.0 collective-permute-start.11
  167.7 10.1 %block_update.1 = (f32[256,128]{1,0:T(8,128)}, f32[256,128]{1,0:T(8,128)S(1)}) custom-call(bf16[256,7168]{1,0:T(8,128)(2,1)} %bitcast.95, s32[1,256]{1,0:T(1,128)S(1)} %copy-done, f32[128]{0:T(128)S(1)} %divide_bitcast_fusion.pivots_ref, f32[128,128]{1,0:T(8,128)S(1)} %copy.13.upper_ref, f32[128,128]{1,0:T(8,128)S(1)} %get-tuple-element.154.turned_ref), custom_call_target="tpu_custom_call" | custom-call | flops 1000000000 | bytes 2000000 | tf_op jit(solution)/shard_map/block_update/pallas_call | solution.py:485
  177.8 1.5 fusion.16
  179.2 5.2 %collective-permute-done.10 = f16[1552,128]{1,0:T(8,128)(2,1)S(1)} collective-permute-done((f16[1552,128]{1,0:T(8,128)(2,1)}, f16[1552,128]{1,0:T(8,128)(2,1)S(1)}, u32[]{:S(2)}, u32[]{:S(2)}) %collective-permute-start.10) | collective-permute-done | bytes 397344 | tf_op jit(solution)/shard_map/ppermute | solution.py:412
  184.4 3.4 %collective-permute-done.12 = f16[1552,128]{1,0:T(8,128)(2,1)S(1)} collective-permute-done((f16[1552,128]{1,0:T(8,128)(2,1)S(1)}, f16[1552,128]{1,0:T(8,128)(2,1)S(1)}, u32[]{:S(2)}, u32[]{:S(2)}) %collective-permute-start.12) | collective-permute-done | bytes 397344 | tf_op jit(solution)/shard_map/ppermute | solution.py:412
  188.2 1.3 pad_maximum_fusion
  189.5 6.7 %all-to-all-start.2 = ((f16[16,240,128]{2,1,0:T(8,128)(2,1)}), f16[16,240,128]{2,1,0:T(8,128)(2,1)S(1)}, u32[]{:S(2)}, u32[]{:S(2)}) async-start(f16[16,240,128]{2,1,0:T(8,128)(2,1)} %pad_maximum_fusion), calls=%async_computation.2 | async-start | bytes 1966080 | tf_op jit(solution)/shard_map/all_to_all | solution.py:607
  196.2 0.7 fusion.33
  196.8 11.2 %later_columns.1 = f32[256,7040]{1,0:T(8,128)} custom-call(s32[2]{0:T(128)S(1)} %pad_add_fusion.here_ref, f32[256,128]{1,0:T(8,128)S(1)} %get-tuple-element.129.errors_ref, bf16[4,880,128]{2,1,0:T(8,128)(2,1)S(1)} %pad_maximum_fusion.1.own_ref, bf16[4,880,128]{2,1,0:T(8,128)(2,1)S(1)} %collective-permute-done.13.other_ref, bf16[256,7168]{1,0:T(8,128)(2,1)} %bitcast.96, ...), custom_call_target="tpu_custom_call" | custom-call | flops 1500000000 | bytes 13000000 | tf_op jit(solution)/shard_map/later_columns/pallas_call | solution.py:547
  208.1 5.1 %all-to-all-done.2 = f16[16,240,128]{2,1,0:T(8,128)(2,1)S(1)} async-done(((f16[16,240,128]{2,1,0:T(8,128)(2,1)}), f16[16,240,128]{2,1,0:T(8,128)(2,1)S(1)}, u32[]{:S(2)}, u32[]{:S(2)}) %all-to-all-start.2) | async-done | bytes 983072 | tf_op jit(solution)/shard_map/all_to_all | solution.py:607
  213.4 2.2 put_in_order.1
  (50 shorter events, 3.8 us)
Async XLA Ops:
  90.4 26.3 %all-to-all-start.1 = ((bf16[16,384,128]{2,1,0:T(8,128)(2,1)}), bf16[16,384,128]{2,1,0:T(8,128)(2,1)S(1)}, u32[]{:S(2)}, u32[]{:S(2)}) async-start(bf16[16,384,128]{2,1,0:T(8,128)(2,1)} %get-tuple-element.76), calls=%async_computation.1 | async-start | bytes 3145728 | tf_op jit(solution)/shard_map/all_to_all | solution.py:578
  94.1 23.1 %copy-start.3 = (f32[1,128,880]{1,2,0:T(8,128)S(1)}, f32[1,128,880]{1,2,0:T(8,128)}, u32[]{:S(2)}) copy-start(f32[1,128,880]{1,2,0:T(8,128)} %param.13) | copy-start | bytes 1351684
  116.7 7.4 %collective-permute-start.1 = (f32[4,2064,128]{2,1,0:T(8,128)}, f32[4,2064,128]{2,1,0:T(8,128)S(1)}, u32[]{:S(2)}, u32[]{:S(2)}) collective-permute-start(f32[4,2064,128]{2,1,0:T(8,128)} %get-tuple-element.85), channel_id=1, source_target_pairs={{0,16},{16,0},{1,17},{17,1},{2,18},{18,2},{3,19},{19,3},{4,20},{20... | collective-permute-start | bytes 12681224 | tf_op jit(solution)/shard_map/ppermute | solution.py:383
  116.7 5.9 %collective-permute-start = (f32[8,128]{1,0:T(8,128)S(1)}, f32[8,128]{1,0:T(8,128)S(1)}, u32[]{:S(2)}, u32[]{:S(2)}) collective-permute-start(f32[8,128]{1,0:T(8,128)S(1)} %get-tuple-element.80), channel_id=1, source_target_pairs={{0,16},{16,0},{1,17},{17,1},{2,18},{18,2},{3,19},{19,3},{4,20},{20... | collective-permute-start | bytes 12296 | tf_op jit(solution)/shard_map/ppermute | solution.py:383
  117.2 13.6 %collective-permute-start.5 = (bf16[880,128]{1,0:T(8,128)(2,1)S(1)}, bf16[880,128]{1,0:T(8,128)(2,1)S(1)}, u32[]{:S(2)}, u32[]{:S(2)}) collective-permute-start(bf16[880,128]{1,0:T(8,128)(2,1)S(1)} %convert_bitcast_fusion), channel_id=1, source_target_pairs={{0,96},{32,0},{64,32},{96,64},{1,97},{33,1},{65,33},{97,65},{2,98}... | collective-permute-start | bytes 675848 | tf_op jit(solution)/shard_map/ppermute | solution.py:505
  118.1 25.9 %collective-permute-start.6 = (bf16[880,128]{1,0:T(8,128)(2,1)S(1)}, bf16[880,128]{1,0:T(8,128)(2,1)S(1)}, u32[]{:S(2)}, u32[]{:S(2)}) collective-permute-start(bf16[880,128]{1,0:T(8,128)(2,1)S(1)} %convert_bitcast_fusion), channel_id=1, source_target_pairs={{0,64},{32,96},{64,0},{96,32},{1,65},{33,97},{65,1},{97,33},{2,66}... | collective-permute-start | bytes 675848 | tf_op jit(solution)/shard_map/ppermute | solution.py:505
  119.2 24.8 %collective-permute-start.7 = (bf16[880,128]{1,0:T(8,128)(2,1)S(1)}, bf16[880,128]{1,0:T(8,128)(2,1)S(1)}, u32[]{:S(2)}, u32[]{:S(2)}) collective-permute-start(bf16[880,128]{1,0:T(8,128)(2,1)S(1)} %convert_bitcast_fusion), channel_id=1, source_target_pairs={{0,32},{32,64},{64,96},{96,0},{1,33},{33,65},{65,97},{97,1},{2,34}... | collective-permute-start | bytes 675848 | tf_op jit(solution)/shard_map/ppermute | solution.py:505
  127.6 27.2 %copy-start.5 = (f32[1,128]{1,0:T(1,128)S(1)}, f32[1,128]{1,0:T(1,128)}, u32[]{:S(2)}) copy-start(f32[1,128]{1,0:T(1,128)} %param.11) | copy-start | bytes 1540
  127.6 16.5 %collective-permute-start.2 = (f16[2064,128]{1,0:T(8,128)(2,1)S(1)}, f16[2064,128]{1,0:T(8,128)(2,1)S(1)}, u32[]{:S(2)}, u32[]{:S(2)}) collective-permute-start(f16[2064,128]{1,0:T(8,128)(2,1)S(1)} %get-tuple-element.94), channel_id=1, source_target_pairs={{0,32},{32,64},{64,96},{96,0},{1,33},{33,65},{65,97},{97,1},{2,34}... | collective-permute-start | bytes 1585160 | tf_op jit(solution)/shard_map/ppermute | solution.py:412
  128.1 16.4 %collective-permute-start.3 = (f16[2064,128]{1,0:T(8,128)(2,1)S(1)}, f16[2064,128]{1,0:T(8,128)(2,1)S(1)}, u32[]{:S(2)}, u32[]{:S(2)}) collective-permute-start(f16[2064,128]{1,0:T(8,128)(2,1)S(1)} %get-tuple-element.95), channel_id=1, source_target_pairs={{0,64},{32,96},{64,0},{96,32},{1,65},{33,97},{65,1},{97,33},{2,66}... | collective-permute-start | bytes 1585160 | tf_op jit(solution)/shard_map/ppermute | solution.py:412
  130.8 23.9 %collective-permute-start.4 = (f16[2064,128]{1,0:T(8,128)(2,1)S(1)}, f16[2064,128]{1,0:T(8,128)(2,1)S(1)}, u32[]{:S(2)}, u32[]{:S(2)}) collective-permute-start(f16[2064,128]{1,0:T(8,128)(2,1)S(1)} %get-tuple-element.96), channel_id=1, source_target_pairs={{0,96},{32,0},{64,32},{96,64},{1,97},{33,1},{65,33},{97,65},{2,98}... | collective-permute-start | bytes 1585160 | tf_op jit(solution)/shard_map/ppermute | solution.py:412
  154.7 5.9 %collective-permute-start.8 = (f32[4,1552,128]{2,1,0:T(8,128)}, f32[4,1552,128]{2,1,0:T(8,128)S(1)}, u32[]{:S(2)}, u32[]{:S(2)}) collective-permute-start(f32[4,1552,128]{2,1,0:T(8,128)} %get-tuple-element.104), channel_id=1, source_target_pairs={{0,16},{16,0},{1,17},{17,1},{2,18},{18,2},{3,19},{19,3},{4,20},{20... | collective-permute-start | bytes 9535496 | tf_op jit(solution)/shard_map/ppermute | solution.py:383
  154.8 5.9 %copy-start.1 = (f32[4,1552,128]{2,1,0:T(8,128)S(1)}, f32[4,1552,128]{2,1,0:T(8,128)}, u32[]{:S(2)}) copy-start(f32[4,1552,128]{2,1,0:T(8,128)} %get-tuple-element.103) | copy-start | bytes 9535492
  156.3 4.2 %collective-permute-start.9 = (f32[8,128]{1,0:T(8,128)S(1)}, f32[8,128]{1,0:T(8,128)S(1)}, u32[]{:S(2)}, u32[]{:S(2)}) collective-permute-start(f32[8,128]{1,0:T(8,128)S(1)} %get-tuple-element.105), channel_id=1, source_target_pairs={{0,16},{16,0},{1,17},{17,1},{2,18},{18,2},{3,19},{19,3},{4,20},{20... | collective-permute-start | bytes 12296 | tf_op jit(solution)/shard_map/ppermute | solution.py:383
  160.6 2.6 %copy-start.2 = (f32[4,1552,128]{2,1,0:T(8,128)}, f32[4,1552,128]{2,1,0:T(8,128)S(1)}, u32[]{:S(2)}) copy-start(f32[4,1552,128]{2,1,0:T(8,128)S(1)} %collective-permute-done.8) | copy-start | bytes 9535492
  163.2 24.5 %collective-permute-start.13 = (bf16[4,880,128]{2,1,0:T(8,128)(2,1)S(1)}, bf16[4,880,128]{2,1,0:T(8,128)(2,1)S(1)}, u32[]{:S(2)}, u32[]{:S(2)}) collective-permute-start(bf16[4,880,128]{2,1,0:T(8,128)(2,1)S(1)} %pad_maximum_fusion.1.own_ref), channel_id=1, source_target_pairs={{0,16},{16,0},{1,17},{17,1},{2,18},{18,2},{3,19},{19,3},{4,20},{20... | collective-permute-start | bytes 2703368 | tf_op jit(solution)/shard_map/ppermute | solution.py:599
  163.4 0.8 copy-start.4
  163.4 4.3 %copy-start = (s32[1,256]{1,0:T(1,128)S(1)}, s32[1,256]{1,0:T(1,128)}, u32[]{:S(2)}) copy-start(s32[1,256]{1,0:T(1,128)} %levels_ref) | copy-start | bytes 3076
  164.4 20.0 %collective-permute-start.10 = (f16[1552,128]{1,0:T(8,128)(2,1)}, f16[1552,128]{1,0:T(8,128)(2,1)S(1)}, u32[]{:S(2)}, u32[]{:S(2)}) collective-permute-start(f16[1552,128]{1,0:T(8,128)(2,1)} %get-tuple-element.114), channel_id=1, source_target_pairs={{0,32},{32,64},{64,96},{96,0},{1,33},{33,65},{65,97},{97,1},{2,34}... | collective-permute-start | bytes 1191944 | tf_op jit(solution)/shard_map/ppermute | solution.py:412
  166.6 17.9 %collective-permute-start.11 = (f16[1552,128]{1,0:T(8,128)(2,1)S(1)}, f16[1552,128]{1,0:T(8,128)(2,1)S(1)}, u32[]{:S(2)}, u32[]{:S(2)}) collective-permute-start(f16[1552,128]{1,0:T(8,128)(2,1)S(1)} %get-tuple-element.115), channel_id=1, source_target_pairs={{0,64},{32,96},{64,0},{96,32},{1,65},{33,97},{65,1},{97,33},{2,66}... | collective-permute-start | bytes 1191944 | tf_op jit(solution)/shard_map/ppermute | solution.py:412
  167.5 20.2 %collective-permute-start.12 = (f16[1552,128]{1,0:T(8,128)(2,1)S(1)}, f16[1552,128]{1,0:T(8,128)(2,1)S(1)}, u32[]{:S(2)}, u32[]{:S(2)}) collective-permute-start(f16[1552,128]{1,0:T(8,128)(2,1)S(1)} %get-tuple-element.116), channel_id=1, source_target_pairs={{0,96},{32,0},{64,32},{96,64},{1,97},{33,1},{65,33},{97,65},{2,98}... | collective-permute-start | bytes 1191944 | tf_op jit(solution)/shard_map/ppermute | solution.py:412
  189.5 23.7 %all-to-all-start.2 = ((f16[16,240,128]{2,1,0:T(8,128)(2,1)}), f16[16,240,128]{2,1,0:T(8,128)(2,1)S(1)}, u32[]{:S(2)}, u32[]{:S(2)}) async-start(f16[16,240,128]{2,1,0:T(8,128)(2,1)} %pad_maximum_fusion), calls=%async_computation.2 | async-start | bytes 1966080 | tf_op jit(solution)/shard_map/all_to_all | solution.py:607

commit v3 on v2

--- a/solution.py
+++ b/solution.py
@@ -49,6 +49,9 @@
 
 def build_kernel(tokens_ref, routes_ref, first_ref, second_ref, slab):
     i = pl.program_id(0)
+    routes = routes_ref[...].astype(f32)
+    halves = [routes[k : k + 1, at : at + 128] for k in range(2) for at in (0, 128)]
+    routes_rows = jnp.concatenate([*halves, jnp.zeros((ROUTE_ROWS - 4, 128), f32)], axis=0).astype(bf16)
 
     @pl.when(i == 0)
     def _():
@@ -66,7 +69,7 @@
     for half, (left, right) in enumerate(((last, turned), (turned, last))):
         to = 2 * i + half
         first_ref[half, :SLAB_ROWS, :] = slab[...]
-        first_ref[half, SLAB_ROWS : SLAB_ROWS + ROUTE_ROWS, :] = routes_ref[...]
+        first_ref[half, SLAB_ROWS : SLAB_ROWS + ROUTE_ROWS, :] = routes_rows
         start = SLAB_ROWS + ROUTE_ROWS
         first_ref[half, start : start + TOK, :] = tile(to)
         first_ref[half, start + TOK : start + 2 * TOK, :] = tile(EXPERTS + to)
@@ -74,13 +77,13 @@
         second_ref[half, TOK:, :] = jnp.where(low, left[:128], right[128:]).astype(bf16)
 
 
-def build(tokens, routes_rows):
+def build(tokens, routes):
     return pl.pallas_call(
         build_kernel,
         grid=(EXPERTS // 2,),
         in_specs=[
             pl.BlockSpec((TOK, tokens.shape[1]), lambda i: (0, 0)),
-            pl.BlockSpec((ROUTE_ROWS, 128), lambda i: (0, 0)),
+            pl.BlockSpec((2, TOK), lambda i: (0, 0)),
         ],
         out_specs=[
             pl.BlockSpec((2, FIRST_ROWS, 128), lambda i: (i, 0, 0)),
@@ -93,7 +96,7 @@
         scratch_shapes=[pltpu.VMEM((SLAB_ROWS, 128), bf16)],
         compiler_params=pltpu.CompilerParams(vmem_limit_bytes=24 * MIB),
         name="build",
-    )(pltpu.with_memory_space_constraint(tokens, pltpu.HBM), routes_rows)
+    )(pltpu.with_memory_space_constraint(tokens, pltpu.HBM), routes)
 
 
 def places_of(routes_rows):
@@ -438,7 +441,9 @@
     )(scale, a, b)
 
 
-def columns_kernel(block_ref, levels_ref, pivots_ref, upper_ref, turned_ref, snapped_ref, errors_ref, now, out, err):
+def columns_kernel(
+    block_ref, levels_ref, pivots_ref, diag_ref, snapped_ref, errors_ref, now, out, err, upper_ref, turned_ref
+):
     block = block_ref[...].astype(f32).T
     now[...] = block
     largest = jnp.max(jnp.abs(block), axis=0, keepdims=True)
@@ -446,6 +451,10 @@
     per_turn = 1.0 / spacing
     reach = 0.9 * spacing / (2.0 * math.pi)
     lane = lax.broadcasted_iota(i32, (8, BLOCK), 1)
+    row, column = (lax.broadcasted_iota(i32, (BLOCK, BLOCK), d) for d in range(2))
+    upper = jnp.where(column > row, diag_ref[...], 0.0)
+    upper_ref[...] = upper
+    turned_ref[...] = upper.T
 
     def group(b, carry):
         at = pl.multiple_of(b * 8, 8)
@@ -479,7 +488,7 @@
     errors_ref[...] = err[...].T
 
 
-def block_update(rows, levels, pivots, upper):
+def block_update(rows, levels, pivots, panel_diag):
     whole = lambda *shape: pl.BlockSpec(shape, lambda i: (0,) * len(shape))
     count = rows.shape[0]
     return pl.pallas_call(
@@ -490,15 +499,14 @@
             whole(1, count),
             pl.BlockSpec(memory_space=pltpu.SMEM),
             whole(BLOCK, BLOCK),
-            whole(BLOCK, BLOCK),
         ],
         out_specs=[whole(count, BLOCK)] * 2,
         out_shape=[jax.ShapeDtypeStruct((count, BLOCK), f32)] * 2,
-        scratch_shapes=[pltpu.VMEM((BLOCK, count), f32)] * 3,
+        scratch_shapes=[pltpu.VMEM((BLOCK, count), f32)] * 3 + [pltpu.VMEM((BLOCK, BLOCK), f32)] * 2,
         compiler_params=pltpu.CompilerParams(vmem_limit_bytes=16 * MIB),
         cost_estimate=pl.CostEstimate(flops=10**9, bytes_accessed=2 * 10**6, transcendentals=0),
         name="block_update",
-    )(pltpu.with_memory_space_constraint(rows, pltpu.HBM), levels, 1.0 / pivots, upper, upper.T)
+    )(pltpu.with_memory_space_constraint(rows, pltpu.HBM), levels, 1.0 / pivots, panel_diag)
 
 
 def ahead_over_x(mine):
@@ -563,13 +571,12 @@
 def on_device(tokens, routes, weight, levels, pivots, panel_diag, panel_rest):
     x, core = lax.axis_index("x"), lax.axis_index("core")
     place = lax.axis_index("z") * 4 + lax.axis_index("y")
-    routes_rows = jnp.pad(routes.T.reshape(4, 128).astype(bf16), ((0, ROUTE_ROWS - 4), (0, 0)))
     exchange = functools.partial(
         lax.all_to_all, axis_name=PLANE, split_axis=0, concat_axis=0, tiled=True
     )
     here = jnp.stack([x, core]).astype(i32)
 
-    first, second = build(tokens, routes_rows)
+    first, second = build(tokens, routes.T)
     first, here, place, pivots = lax.optimization_barrier((first, here, place, pivots))
     first = exchange(first)
     first, second, weight, levels, panel_diag, panel_rest, pivots = lax.optimization_barrier(
@@ -588,14 +595,14 @@
     keep, send, top, others, panel, weight = lax.optimization_barrier(
         (keep, send, top, others, panel, weight)
     )
-    total, least, counts = sum_over_x(own, others)
     panel = jnp.stack(panel)
+    far_own, far_others = own, others
     own, others = sum_over_core(keep, *over_core(send, top))
 
-    others, rows, panel_diag, panel = lax.optimization_barrier((others, weight[0], panel_diag, panel))
+    others, rows, panel, far_others = lax.optimization_barrier((others, weight[0], panel, far_others))
     others = over_x(others)
-    upper = jnp.triu(panel_diag[0], 1)
-    snapped, errors = block_update(rows, levels, pivots[0], upper)
+    total, least, counts = sum_over_x(far_own, far_others)
+    snapped, errors = block_update(rows, levels, pivots[0], panel_diag[0])
     other_panel = lax.ppermute(panel, "core", SWAP)
     others, errors, other_panel, total, least = lax.optimization_barrier(
         (others, errors, other_panel, total, least)

time: 217 us -> 215 us (level)
  other arithmetic: 13 us -> 9.61 us
  transfers between devices with their start and end apart: 16 -> 16, of which waited for: 11 -> 11; matrix products, arithmetic and copies ran while one was open for 4% -> 3% of each run, Pallas kernels for 26% -> 26%
where the time goes in v3:
time: 215 us; the launch traced here: 213 us
  blocking collectives  82.2 us (38%)
  Pallas kernels  65.4 us (30%)
  waiting for transfers between devices  32.5 us (15%)
  starting transfers between devices  21.9 us (10%)
  other arithmetic  9.61 us (4%)
    all_to_all x1, blocking collectives, on_device(): first = exchange(first)  82.2 us
    pallas_call x1, Pallas kernels, product0(): pl.pallas_call(product0_kernel, grid_spec=pltpu.PrefetchScalarGridSpec(nu...  21.9 us
    ppermute x6, waiting for transfers between devices, over_x(): lax.ppermute(value, 'x', pairs)  20.1 us
    pallas_call x1, Pallas kernels, product1(): pl.pallas_call(product1_kernel, grid_spec=pltpu.PrefetchScalarGridSpec(nu...  13.2 us
    pallas_call x1, Pallas kernels, later_columns(): pl.pallas_call(later_kernel, grid_spec=pltpu.PrefetchScalarGridSpec(num_s...  11.3 us
    pallas_call x1, Pallas kernels, block_update(): pl.pallas_call(columns_kernel, grid=(1,), in_specs=[whole(count, BLOCK),...  10.1 us
    pallas_call x1, Pallas kernels, build(): pl.pallas_call(build_kernel, grid=(EXPERTS // 2,), in_specs=[pl.BlockSpec...  6.8 us
    all_to_all x1, starting transfers between devices, on_device(): sums = exchange(jnp.concatenate(sent, axis=1))  6.66 us
  transfers between devices with their start and end apart: 16, of which 11 were waited for; matrix products, arithmetic and copies ran while one was open for 3% of the time, Pallas kernels for 26%

profile of v3, /device:TPU:6, one launch (start us, length us, event | category | flops | bytes accessed | tf_op | source)
XLA Modules:
  0.0 213.2 jit_solution(15046704218830211268)
XLA Ops:
  0.7 0.7 copy-done.1
  1.4 6.8 %build.1 = (bf16[16,1552,128]{2,1,0:T(8,128)(2,1)}, bf16[16,384,128]{2,1,0:T(8,128)(2,1)}) custom-call(bf16[256,7168]{1,0:T(8,128)(2,1)} %tokens_ref.1, s32[2,256]{1,0:T(2,128)S(1)} %bitcast.90), custom_call_target="tpu_custom_call" | custom-call | tf_op jit(solution)/shard_map/build/pallas_call | solution.py:81
  8.2 82.2 %all_to_all.15.in_ref = bf16[16,1552,128]{2,1,0:T(8,128)(2,1)} all-to-all(bf16[16,1552,128]{2,1,0:T(8,128)(2,1)} %get-tuple-element.71), channel_id=1, replica_groups=mesh['x'=4,'core'=2,'z'=4,'y'=4] {'z','y'}, dimensions={0} | all-to-all | bytes 12713984 | tf_op jit(solution)/shard_map/all_to_all | solution.py:581
  90.4 3.7 %all-to-all-start.1 = ((bf16[16,384,128]{2,1,0:T(8,128)(2,1)}), bf16[16,384,128]{2,1,0:T(8,128)(2,1)S(1)}, u32[]{:S(2)}, u32[]{:S(2)}) async-start(bf16[16,384,128]{2,1,0:T(8,128)(2,1)} %get-tuple-element.78), calls=%async_computation.1 | async-start | bytes 3145728 | tf_op jit(solution)/shard_map/all_to_all | solution.py:585
  94.1 21.9 %product0.1 = (f32[4,2064,128]{2,1,0:T(8,128)}, f32[4,2064,128]{2,1,0:T(8,128)}, f32[8,128]{1,0:T(8,128)S(1)}, bf16[8,16,512,128]{3,2,1,0:T(8,128)(2,1)}, f32[16,16,256]{2,1,0:T(8,128)S(1)}) custom-call(s32[2]{0:T(128)S(1)} %pad_add_fusion.here_ref, bf16[16,1552,128]{2,1,0:T(8,128)(2,1)} %all_to_all.15.in_ref), custom_call_target="tpu_custom_call" | custom-call | flops 11000000512 | bytes 16000000 | tf_op jit(solution)/shard_map/product0/pallas_call | solution.py:264
  116.1 0.6 all-to-all-done.1.cols_ref
  116.7 0.5 collective-permute-start
  117.2 0.9 collective-permute-start.5
  118.1 1.1 collective-permute-start.6
  119.2 2.1 collective-permute-start.7
  121.3 1.3 collective-permute-done
  122.6 1.5 collective-permute-done.1
  124.1 3.4 %fusion.2 = (f16[2064,128]{1,0:T(8,128)(2,1)S(1)}, f16[2064,128]{1,0:T(8,128)(2,1)S(1)}, f16[2064,128]{1,0:T(8,128)(2,1)S(1)}) fusion(f32[4,2064,128]{2,1,0:T(8,128)S(1)} %collective-permute-done.1, f32[4,2064,128]{2,1,0:T(8,128)} %get-tuple-element.86, f32[128]{0:T(128)S(1)} %bitcast.107, f32[128]{0:T(128)S(1)} %get-tuple-element.159, f32[128]{0:T(128)S(1)} %bitcast.110, ...), kind=kLoop, calls=%fused_computation.8 | loop fusion | flops 3434496 | bytes 7931424 | tf_op jit(solution)/shard_map/convert_element_type | solution.py:397
  127.5 0.5 collective-permute-start.2
  128.1 2.4 %collective-permute-start.3 = (f16[2064,128]{1,0:T(8,128)(2,1)S(1)}, f16[2064,128]{1,0:T(8,128)(2,1)S(1)}, u32[]{:S(2)}, u32[]{:S(2)}) collective-permute-start(f16[2064,128]{1,0:T(8,128)(2,1)S(1)} %get-tuple-element.97), channel_id=1, source_target_pairs={{0,64},{32,96},{64,0},{96,32},{1,65},{33,97},{65,1},{97,33},{2,66}... | collective-permute-start | bytes 1585160 | tf_op jit(solution)/shard_map/ppermute | solution.py:415
  130.8 13.2 %product1.1 = (f32[4,1552,128]{2,1,0:T(8,128)}, f32[4,1552,128]{2,1,0:T(8,128)}, f32[8,128]{1,0:T(8,128)S(1)}) custom-call(s32[2]{0:T(128)S(1)} %pad_add_fusion.here_ref, f32[16,16,256]{2,1,0:T(8,128)S(1)} %get-tuple-element.90.places_ref, bf16[16,384,128]{2,1,0:T(8,128)(2,1)S(1)} %all-to-all-done.1.cols_ref, ...), custom_call_target="tpu_custom_call" | custom-call | flops 11000000512 | bytes 16000000 | tf_op jit(solution)/shard_map/product1/pallas_call | solution.py:358
  144.5 10.2 %collective-permute-done.4 = f16[2064,128]{1,0:T(8,128)(2,1)S(1)} collective-permute-done((f16[2064,128]{1,0:T(8,128)(2,1)S(1)}, f16[2064,128]{1,0:T(8,128)(2,1)S(1)}, u32[]{:S(2)}, u32[]{:S(2)}) %collective-permute-start.4) | collective-permute-done | bytes 528416 | tf_op jit(solution)/shard_map/ppermute | solution.py:415
  154.8 1.5 fusion.3
  156.2 0.6 collective-permute-start.9
  156.9 3.5 %collective-permute-done.9 = f32[8,128]{1,0:T(8,128)S(1)} collective-permute-done((f32[8,128]{1,0:T(8,128)S(1)}, f32[8,128]{1,0:T(8,128)S(1)}, u32[]{:S(2)}, u32[]{:S(2)}) %collective-permute-start.9) | collective-permute-done | bytes 4128 | tf_op jit(solution)/shard_map/ppermute | solution.py:386
  160.6 1.3 fusion.15
  162.1 2.1 collective-permute-start.10
  164.2 1.0 collective-permute-start.11
  165.4 10.1 %block_update.1 = (f32[256,128]{1,0:T(8,128)}, f32[256,128]{1,0:T(8,128)S(1)}) custom-call(bf16[256,7168]{1,0:T(8,128)(2,1)} %bitcast.91, s32[1,256]{1,0:T(1,128)S(1)} %copy-done.2, f32[128]{0:T(128)S(1)} %divide_bitcast_fusion.pivots_ref, f32[128,128]{1,0:T(8,128)S(1)} %bitcast.89), custom_call_target="tpu_custom_call" | custom-call | flops 1000000000 | bytes 2000000 | tf_op jit(solution)/shard_map/block_update/pallas_call | solution.py:494
  176.0 5.8 %collective-permute-done.10 = f16[1552,128]{1,0:T(8,128)(2,1)S(1)} collective-permute-done((f16[1552,128]{1,0:T(8,128)(2,1)S(1)}, f16[1552,128]{1,0:T(8,128)(2,1)S(1)}, u32[]{:S(2)}, u32[]{:S(2)}) %collective-permute-start.10) | collective-permute-done | bytes 397344 | tf_op jit(solution)/shard_map/ppermute | solution.py:415
  181.8 3.7 %collective-permute-done.12 = f16[1552,128]{1,0:T(8,128)(2,1)S(1)} collective-permute-done((f16[1552,128]{1,0:T(8,128)(2,1)S(1)}, f16[1552,128]{1,0:T(8,128)(2,1)S(1)}, u32[]{:S(2)}, u32[]{:S(2)}) %collective-permute-start.12) | collective-permute-done | bytes 397344 | tf_op jit(solution)/shard_map/ppermute | solution.py:415
  185.9 1.3 pad_maximum_fusion
  187.1 6.7 %all-to-all-start.2 = ((f16[16,240,128]{2,1,0:T(8,128)(2,1)}), f16[16,240,128]{2,1,0:T(8,128)(2,1)S(1)}, u32[]{:S(2)}, u32[]{:S(2)}) async-start(f16[16,240,128]{2,1,0:T(8,128)(2,1)} %pad_maximum_fusion), calls=%async_computation.2 | async-start | bytes 1966080 | tf_op jit(solution)/shard_map/all_to_all | solution.py:614
  193.8 0.7 fusion.32
  194.5 11.3 %later_columns.1 = f32[256,7040]{1,0:T(8,128)} custom-call(s32[2]{0:T(128)S(1)} %pad_add_fusion.here_ref, f32[256,128]{1,0:T(8,128)S(1)} %get-tuple-element.133.errors_ref, bf16[4,880,128]{2,1,0:T(8,128)(2,1)S(1)} %pad_maximum_fusion.1.own_ref, bf16[4,880,128]{2,1,0:T(8,128)(2,1)S(1)} %collective-permute-done.13.other_ref, bf16[256,7168]{1,0:T(8,128)(2,1)} %bitcast.92, ...), custom_call_target="tpu_custom_call" | custom-call | flops 1500000000 | bytes 13000000 | tf_op jit(solution)/shard_map/later_columns/pallas_call | solution.py:555
  205.7 5.1 %all-to-all-done.2 = f16[16,240,128]{2,1,0:T(8,128)(2,1)S(1)} async-done(((f16[16,240,128]{2,1,0:T(8,128)(2,1)}), f16[16,240,128]{2,1,0:T(8,128)(2,1)S(1)}, u32[]{:S(2)}, u32[]{:S(2)}) %all-to-all-start.2) | async-done | bytes 983072 | tf_op jit(solution)/shard_map/all_to_all | solution.py:614
  211.0 2.1 %put_in_order.1 = f32[64,7168]{1,0:T(8,128)} custom-call(f32[1]{0:T(128)} %bitcast.23.scale_ref, f32[16,128,128]{2,1,0:T(8,128)S(1)} %convert_multiply_fusion.a_ref, f32[16,96,128]{2,1,0:T(8,128)S(1)} %convert_multiply_fusion.1.b_ref), custom_call_target="tpu_custom_call" | custom-call | tf_op jit(solution)/shard_map/put_in_order/pallas_call | solution.py:434
  (44 shorter events, 2.9 us)
Async XLA Ops:
  0.7 0.7 copy-start.1
  90.4 26.3 %all-to-all-start.1 = ((bf16[16,384,128]{2,1,0:T(8,128)(2,1)}), bf16[16,384,128]{2,1,0:T(8,128)(2,1)S(1)}, u32[]{:S(2)}, u32[]{:S(2)}) async-start(bf16[16,384,128]{2,1,0:T(8,128)(2,1)} %get-tuple-element.78), calls=%async_computation.1 | async-start | bytes 3145728 | tf_op jit(solution)/shard_map/all_to_all | solution.py:585
  94.1 23.1 %copy-start.4 = (f32[1,128,880]{1,2,0:T(8,128)S(1)}, f32[1,128,880]{1,2,0:T(8,128)}, u32[]{:S(2)}) copy-start(f32[1,128,880]{1,2,0:T(8,128)} %param.13) | copy-start | bytes 1351684
  116.7 7.4 %collective-permute-start.1 = (f32[4,2064,128]{2,1,0:T(8,128)}, f32[4,2064,128]{2,1,0:T(8,128)S(1)}, u32[]{:S(2)}, u32[]{:S(2)}) collective-permute-start(f32[4,2064,128]{2,1,0:T(8,128)} %get-tuple-element.87), channel_id=1, source_target_pairs={{0,16},{16,0},{1,17},{17,1},{2,18},{18,2},{3,19},{19,3},{4,20},{20... | collective-permute-start | bytes 12681224 | tf_op jit(solution)/shard_map/ppermute | solution.py:386
  116.7 5.9 %collective-permute-start = (f32[8,128]{1,0:T(8,128)S(1)}, f32[8,128]{1,0:T(8,128)S(1)}, u32[]{:S(2)}, u32[]{:S(2)}) collective-permute-start(f32[8,128]{1,0:T(8,128)S(1)} %get-tuple-element.82), channel_id=1, source_target_pairs={{0,16},{16,0},{1,17},{17,1},{2,18},{18,2},{3,19},{19,3},{4,20},{20... | collective-permute-start | bytes 12296 | tf_op jit(solution)/shard_map/ppermute | solution.py:386
  117.2 13.6 %collective-permute-start.5 = (bf16[880,128]{1,0:T(8,128)(2,1)S(1)}, bf16[880,128]{1,0:T(8,128)(2,1)S(1)}, u32[]{:S(2)}, u32[]{:S(2)}) collective-permute-start(bf16[880,128]{1,0:T(8,128)(2,1)S(1)} %convert_bitcast_fusion), channel_id=1, source_target_pairs={{0,96},{32,0},{64,32},{96,64},{1,97},{33,1},{65,33},{97,65},{2,98}... | collective-permute-start | bytes 675848 | tf_op jit(solution)/shard_map/ppermute | solution.py:513
  118.1 25.9 %collective-permute-start.6 = (bf16[880,128]{1,0:T(8,128)(2,1)S(1)}, bf16[880,128]{1,0:T(8,128)(2,1)S(1)}, u32[]{:S(2)}, u32[]{:S(2)}) collective-permute-start(bf16[880,128]{1,0:T(8,128)(2,1)S(1)} %convert_bitcast_fusion), channel_id=1, source_target_pairs={{0,64},{32,96},{64,0},{96,32},{1,65},{33,97},{65,1},{97,33},{2,66}... | collective-permute-start | bytes 675848 | tf_op jit(solution)/shard_map/ppermute | solution.py:513
  119.2 24.8 %collective-permute-start.7 = (bf16[880,128]{1,0:T(8,128)(2,1)S(1)}, bf16[880,128]{1,0:T(8,128)(2,1)S(1)}, u32[]{:S(2)}, u32[]{:S(2)}) collective-permute-start(bf16[880,128]{1,0:T(8,128)(2,1)S(1)} %convert_bitcast_fusion), channel_id=1, source_target_pairs={{0,32},{32,64},{64,96},{96,0},{1,33},{33,65},{65,97},{97,1},{2,34}... | collective-permute-start | bytes 675848 | tf_op jit(solution)/shard_map/ppermute | solution.py:513
  127.5 27.2 %copy-start.5 = (f32[1,128]{1,0:T(1,128)S(1)}, f32[1,128]{1,0:T(1,128)}, u32[]{:S(2)}) copy-start(f32[1,128]{1,0:T(1,128)} %param.11) | copy-start | bytes 1540
  127.5 16.5 %collective-permute-start.2 = (f16[2064,128]{1,0:T(8,128)(2,1)S(1)}, f16[2064,128]{1,0:T(8,128)(2,1)S(1)}, u32[]{:S(2)}, u32[]{:S(2)}) collective-permute-start(f16[2064,128]{1,0:T(8,128)(2,1)S(1)} %get-tuple-element.96), channel_id=1, source_target_pairs={{0,32},{32,64},{64,96},{96,0},{1,33},{33,65},{65,97},{97,1},{2,34}... | collective-permute-start | bytes 1585160 | tf_op jit(solution)/shard_map/ppermute | solution.py:415
  128.1 16.4 %collective-permute-start.3 = (f16[2064,128]{1,0:T(8,128)(2,1)S(1)}, f16[2064,128]{1,0:T(8,128)(2,1)S(1)}, u32[]{:S(2)}, u32[]{:S(2)}) collective-permute-start(f16[2064,128]{1,0:T(8,128)(2,1)S(1)} %get-tuple-element.97), channel_id=1, source_target_pairs={{0,64},{32,96},{64,0},{96,32},{1,65},{33,97},{65,1},{97,33},{2,66}... | collective-permute-start | bytes 1585160 | tf_op jit(solution)/shard_map/ppermute | solution.py:415
  130.8 23.9 %collective-permute-start.4 = (f16[2064,128]{1,0:T(8,128)(2,1)S(1)}, f16[2064,128]{1,0:T(8,128)(2,1)S(1)}, u32[]{:S(2)}, u32[]{:S(2)}) collective-permute-start(f16[2064,128]{1,0:T(8,128)(2,1)S(1)} %get-tuple-element.98), channel_id=1, source_target_pairs={{0,96},{32,0},{64,32},{96,64},{1,97},{33,1},{65,33},{97,65},{2,98}... | collective-permute-start | bytes 1585160 | tf_op jit(solution)/shard_map/ppermute | solution.py:415
  154.7 5.9 %collective-permute-start.8 = (f32[4,1552,128]{2,1,0:T(8,128)}, f32[4,1552,128]{2,1,0:T(8,128)S(1)}, u32[]{:S(2)}, u32[]{:S(2)}) collective-permute-start(f32[4,1552,128]{2,1,0:T(8,128)} %get-tuple-element.102), channel_id=1, source_target_pairs={{0,16},{16,0},{1,17},{17,1},{2,18},{18,2},{3,19},{19,3},{4,20},{20... | collective-permute-start | bytes 9535496 | tf_op jit(solution)/shard_map/ppermute | solution.py:386
  154.7 5.9 %copy-start.3 = (f32[4,1552,128]{2,1,0:T(8,128)S(1)}, f32[4,1552,128]{2,1,0:T(8,128)}, u32[]{:S(2)}) copy-start(f32[4,1552,128]{2,1,0:T(8,128)} %get-tuple-element.101) | copy-start | bytes 9535492
  156.2 4.2 %collective-permute-start.9 = (f32[8,128]{1,0:T(8,128)S(1)}, f32[8,128]{1,0:T(8,128)S(1)}, u32[]{:S(2)}, u32[]{:S(2)}) collective-permute-start(f32[8,128]{1,0:T(8,128)S(1)} %get-tuple-element.103), channel_id=1, source_target_pairs={{0,16},{16,0},{1,17},{17,1},{2,18},{18,2},{3,19},{19,3},{4,20},{20... | collective-permute-start | bytes 12296 | tf_op jit(solution)/shard_map/ppermute | solution.py:386
  160.6 4.7 %copy-start = (f32[1,128,128]{2,1,0:T(8,128)S(1)}, f32[1,128,128]{2,1,0:T(8,128)}, u32[]{:S(2)}) copy-start(f32[1,128,128]{2,1,0:T(8,128)} %param.12) | copy-start | bytes 196612
  160.6 4.7 %copy-start.2 = (s32[1,256]{1,0:T(1,128)S(1)}, s32[1,256]{1,0:T(1,128)}, u32[]{:S(2)}) copy-start(s32[1,256]{1,0:T(1,128)} %levels_ref) | copy-start | bytes 3076
  161.9 23.5 %collective-permute-start.13 = (bf16[4,880,128]{2,1,0:T(8,128)(2,1)S(1)}, bf16[4,880,128]{2,1,0:T(8,128)(2,1)S(1)}, u32[]{:S(2)}, u32[]{:S(2)}) collective-permute-start(bf16[4,880,128]{2,1,0:T(8,128)(2,1)S(1)} %pad_maximum_fusion.1.own_ref), channel_id=1, source_target_pairs={{0,16},{16,0},{1,17},{17,1},{2,18},{18,2},{3,19},{19,3},{4,20},{20... | collective-permute-start | bytes 2703368 | tf_op jit(solution)/shard_map/ppermute | solution.py:606
  162.1 19.6 %collective-permute-start.10 = (f16[1552,128]{1,0:T(8,128)(2,1)S(1)}, f16[1552,128]{1,0:T(8,128)(2,1)S(1)}, u32[]{:S(2)}, u32[]{:S(2)}) collective-permute-start(f16[1552,128]{1,0:T(8,128)(2,1)S(1)} %get-tuple-element.118), channel_id=1, source_target_pairs={{0,32},{32,64},{64,96},{96,0},{1,33},{33,65},{65,97},{97,1},{2,34}... | collective-permute-start | bytes 1191944 | tf_op jit(solution)/shard_map/ppermute | solution.py:415
  164.2 17.5 %collective-permute-start.11 = (f16[1552,128]{1,0:T(8,128)(2,1)S(1)}, f16[1552,128]{1,0:T(8,128)(2,1)S(1)}, u32[]{:S(2)}, u32[]{:S(2)}) collective-permute-start(f16[1552,128]{1,0:T(8,128)(2,1)S(1)} %get-tuple-element.119), channel_id=1, source_target_pairs={{0,64},{32,96},{64,0},{96,32},{1,65},{33,97},{65,1},{97,33},{2,66}... | collective-permute-start | bytes 1191944 | tf_op jit(solution)/shard_map/ppermute | solution.py:415
  165.2 20.2 %collective-permute-start.12 = (f16[1552,128]{1,0:T(8,128)(2,1)S(1)}, f16[1552,128]{1,0:T(8,128)(2,1)S(1)}, u32[]{:S(2)}, u32[]{:S(2)}) collective-permute-start(f16[1552,128]{1,0:T(8,128)(2,1)S(1)} %get-tuple-element.120), channel_id=1, source_target_pairs={{0,96},{32,0},{64,32},{96,64},{1,97},{33,1},{65,33},{97,65},{2,98}... | collective-permute-start | bytes 1191944 | tf_op jit(solution)/shard_map/ppermute | solution.py:415
  187.1 23.7 %all-to-all-start.2 = ((f16[16,240,128]{2,1,0:T(8,128)(2,1)}), f16[16,240,128]{2,1,0:T(8,128)(2,1)S(1)}, u32[]{:S(2)}, u32[]{:S(2)}) async-start(f16[16,240,128]{2,1,0:T(8,128)(2,1)} %pad_maximum_fusion), calls=%async_computation.2 | async-start | bytes 1966080 | tf_op jit(solution)/shard_map/all_to_all | solution.py:614

commit v4 on v3

--- a/solution.py
+++ b/solution.py
@@ -595,7 +595,6 @@
     keep, send, top, others, panel, weight = lax.optimization_barrier(
         (keep, send, top, others, panel, weight)
     )
-    panel = jnp.stack(panel)
     far_own, far_others = own, others
     own, others = sum_over_core(keep, *over_core(send, top))
 
@@ -603,6 +602,7 @@
     others = over_x(others)
     total, least, counts = sum_over_x(far_own, far_others)
     snapped, errors = block_update(rows, levels, pivots[0], panel_diag[0])
+    panel = jnp.stack(panel)
     other_panel = lax.ppermute(panel, "core", SWAP)
     others, errors, other_panel, total, least = lax.optimization_barrier(
         (others, errors, other_panel, total, least)

time: 215 us -> 215 us (level)
  no operation moved by 1% of the time
where the time goes in v4:
time: 215 us; the launch traced here: 213 us
  blocking collectives  82.2 us (38%)
  Pallas kernels  65.4 us (30%)
  waiting for transfers between devices  32.4 us (15%)
  starting transfers between devices  21.9 us (10%)
  other arithmetic  9.79 us (5%)
    all_to_all x1, blocking collectives, on_device(): first = exchange(first)  82.2 us
    pallas_call x1, Pallas kernels, product0(): pl.pallas_call(product0_kernel, grid_spec=pltpu.PrefetchScalarGridSpec(nu...  21.9 us
    ppermute x6, waiting for transfers between devices, over_x(): lax.ppermute(value, 'x', pairs)  20.1 us
    pallas_call x1, Pallas kernels, product1(): pl.pallas_call(product1_kernel, grid_spec=pltpu.PrefetchScalarGridSpec(nu...  13.2 us
    pallas_call x1, Pallas kernels, later_columns(): pl.pallas_call(later_kernel, grid_spec=pltpu.PrefetchScalarGridSpec(num_s...  11.3 us
    pallas_call x1, Pallas kernels, block_update(): pl.pallas_call(columns_kernel, grid=(1,), in_specs=[whole(count, BLOCK),...  10.1 us
    pallas_call x1, Pallas kernels, build(): pl.pallas_call(build_kernel, grid=(EXPERTS // 2,), in_specs=[pl.BlockSpec...  6.8 us
    all_to_all x1, starting transfers between devices, on_device(): sums = exchange(jnp.concatenate(sent, axis=1))  6.66 us
  transfers between devices with their start and end apart: 16, of which 11 were waited for; matrix products, arithmetic and copies ran while one was open for 3% of the time, Pallas kernels for 26%

profile of v4, /device:TPU:6, one launch (start us, length us, event | category | flops | bytes accessed | tf_op | source)
XLA Modules:
  0.0 213.3 jit_solution(7953275857819178215)
XLA Ops:
  0.7 0.7 copy-done.1
  1.4 6.8 %build.1 = (bf16[16,1552,128]{2,1,0:T(8,128)(2,1)}, bf16[16,384,128]{2,1,0:T(8,128)(2,1)}) custom-call(bf16[256,7168]{1,0:T(8,128)(2,1)} %tokens_ref.1, s32[2,256]{1,0:T(2,128)S(1)} %bitcast.90), custom_call_target="tpu_custom_call" | custom-call | tf_op jit(solution)/shard_map/build/pallas_call | solution.py:81
  8.2 82.2 %all_to_all.15.in_ref = bf16[16,1552,128]{2,1,0:T(8,128)(2,1)} all-to-all(bf16[16,1552,128]{2,1,0:T(8,128)(2,1)} %get-tuple-element.74), channel_id=1, replica_groups=mesh['x'=4,'core'=2,'z'=4,'y'=4] {'z','y'}, dimensions={0} | all-to-all | bytes 12713984 | tf_op jit(solution)/shard_map/all_to_all | solution.py:581
  90.4 3.7 %all-to-all-start.1 = ((bf16[16,384,128]{2,1,0:T(8,128)(2,1)}), bf16[16,384,128]{2,1,0:T(8,128)(2,1)S(1)}, u32[]{:S(2)}, u32[]{:S(2)}) async-start(bf16[16,384,128]{2,1,0:T(8,128)(2,1)} %get-tuple-element.81), calls=%async_computation.1 | async-start | bytes 3145728 | tf_op jit(solution)/shard_map/all_to_all | solution.py:585
  94.1 21.9 %product0.1 = (f32[4,2064,128]{2,1,0:T(8,128)}, f32[4,2064,128]{2,1,0:T(8,128)}, f32[8,128]{1,0:T(8,128)S(1)}, bf16[8,16,512,128]{3,2,1,0:T(8,128)(2,1)}, f32[16,16,256]{2,1,0:T(8,128)S(1)}) custom-call(s32[2]{0:T(128)S(1)} %pad_add_fusion.here_ref, bf16[16,1552,128]{2,1,0:T(8,128)(2,1)} %all_to_all.15.in_ref), custom_call_target="tpu_custom_call" | custom-call | flops 11000000512 | bytes 16000000 | tf_op jit(solution)/shard_map/product0/pallas_call | solution.py:264
  116.1 0.6 all-to-all-done.1.cols_ref
  117.2 0.9 collective-permute-start.5
  118.1 1.1 collective-permute-start.6
  119.2 2.1 collective-permute-start.7
  121.3 1.3 collective-permute-done
  122.6 1.5 collective-permute-done.1
  124.1 3.5 %fusion.2 = (f16[2064,128]{1,0:T(8,128)(2,1)S(1)}, f16[2064,128]{1,0:T(8,128)(2,1)S(1)}, f16[2064,128]{1,0:T(8,128)(2,1)S(1)}) fusion(f32[4,2064,128]{2,1,0:T(8,128)S(1)} %collective-permute-done.1, f32[4,2064,128]{2,1,0:T(8,128)} %get-tuple-element.89, f32[128]{0:T(128)S(1)} %bitcast.107, f32[128]{0:T(128)S(1)} %get-tuple-element.165, f32[128]{0:T(128)S(1)} %bitcast.110, ...), kind=kLoop, calls=%fused_computation.8 | loop fusion | flops 3434496 | bytes 7931424 | tf_op jit(solution)/shard_map/convert_element_type | solution.py:397
  127.6 0.5 collective-permute-start.2
  128.1 2.4 %collective-permute-start.3 = (f16[2064,128]{1,0:T(8,128)(2,1)S(1)}, f16[2064,128]{1,0:T(8,128)(2,1)S(1)}, u32[]{:S(2)}, u32[]{:S(2)}) collective-permute-start(f16[2064,128]{1,0:T(8,128)(2,1)S(1)} %get-tuple-element.100), channel_id=1, source_target_pairs={{0,64},{32,96},{64,0},{96,32},{1,65},{33,97},{65,1},{97,33},{2,66}... | collective-permute-start | bytes 1585160 | tf_op jit(solution)/shard_map/ppermute | solution.py:415
  130.8 13.2 %product1.1 = (f32[4,1552,128]{2,1,0:T(8,128)}, f32[4,1552,128]{2,1,0:T(8,128)}, f32[8,128]{1,0:T(8,128)S(1)}) custom-call(s32[2]{0:T(128)S(1)} %pad_add_fusion.here_ref, f32[16,16,256]{2,1,0:T(8,128)S(1)} %get-tuple-element.93.places_ref, bf16[16,384,128]{2,1,0:T(8,128)(2,1)S(1)} %all-to-all-done.1.cols_ref, ...), custom_call_target="tpu_custom_call" | custom-call | flops 11000000512 | bytes 16000000 | tf_op jit(solution)/shard_map/product1/pallas_call | solution.py:358
  144.6 10.2 %collective-permute-done.4 = f16[2064,128]{1,0:T(8,128)(2,1)S(1)} collective-permute-done((f16[2064,128]{1,0:T(8,128)(2,1)S(1)}, f16[2064,128]{1,0:T(8,128)(2,1)S(1)}, u32[]{:S(2)}, u32[]{:S(2)}) %collective-permute-start.4) | collective-permute-done | bytes 528416 | tf_op jit(solution)/shard_map/ppermute | solution.py:415
  154.8 0.6 collective-permute-start.9
  155.4 1.7 fusion.3
  157.1 3.0 %collective-permute-done.9 = f32[8,128]{1,0:T(8,128)S(1)} collective-permute-done((f32[8,128]{1,0:T(8,128)S(1)}, f32[8,128]{1,0:T(8,128)S(1)}, u32[]{:S(2)}, u32[]{:S(2)}) %collective-permute-start.9) | collective-permute-done | bytes 4128 | tf_op jit(solution)/shard_map/ppermute | solution.py:386
  160.1 0.5 collective-permute-done.8
  160.6 1.3 fusion.15
  162.3 2.1 collective-permute-start.10
  164.3 1.0 collective-permute-start.11
  165.5 10.1 %block_update.1 = (f32[256,128]{1,0:T(8,128)}, f32[256,128]{1,0:T(8,128)S(1)}) custom-call(bf16[256,7168]{1,0:T(8,128)(2,1)} %bitcast.91, s32[1,256]{1,0:T(1,128)S(1)} %copy-done.2, f32[128]{0:T(128)S(1)} %divide_bitcast_fusion.pivots_ref, f32[128,128]{1,0:T(8,128)S(1)} %bitcast.89), custom_call_target="tpu_custom_call" | custom-call | flops 1000000000 | bytes 2000000 | tf_op jit(solution)/shard_map/block_update/pallas_call | solution.py:494
  176.1 5.8 %collective-permute-done.10 = f16[1552,128]{1,0:T(8,128)(2,1)S(1)} collective-permute-done((f16[1552,128]{1,0:T(8,128)(2,1)S(1)}, f16[1552,128]{1,0:T(8,128)(2,1)S(1)}, u32[]{:S(2)}, u32[]{:S(2)}) %collective-permute-start.10) | collective-permute-done | bytes 397344 | tf_op jit(solution)/shard_map/ppermute | solution.py:415
  181.9 3.7 %collective-permute-done.12 = f16[1552,128]{1,0:T(8,128)(2,1)S(1)} collective-permute-done((f16[1552,128]{1,0:T(8,128)(2,1)S(1)}, f16[1552,128]{1,0:T(8,128)(2,1)S(1)}, u32[]{:S(2)}, u32[]{:S(2)}) %collective-permute-start.12) | collective-permute-done | bytes 397344 | tf_op jit(solution)/shard_map/ppermute | solution.py:415
  186.0 1.3 pad_maximum_fusion
  187.2 6.7 %all-to-all-start.2 = ((f16[16,240,128]{2,1,0:T(8,128)(2,1)}), f16[16,240,128]{2,1,0:T(8,128)(2,1)S(1)}, u32[]{:S(2)}, u32[]{:S(2)}) async-start(f16[16,240,128]{2,1,0:T(8,128)(2,1)} %pad_maximum_fusion), calls=%async_computation.2 | async-start | bytes 1966080 | tf_op jit(solution)/shard_map/all_to_all | solution.py:614
  193.9 0.7 fusion.32
  194.6 11.3 %later_columns.1 = f32[256,7040]{1,0:T(8,128)} custom-call(s32[2]{0:T(128)S(1)} %pad_add_fusion.here_ref, f32[256,128]{1,0:T(8,128)S(1)} %get-tuple-element.139.errors_ref, bf16[4,880,128]{2,1,0:T(8,128)(2,1)S(1)} %pad_maximum_fusion.1.own_ref, bf16[4,880,128]{2,1,0:T(8,128)(2,1)S(1)} %collective-permute-done.13.other_ref, bf16[256,7168]{1,0:T(8,128)(2,1)} %bitcast.92, ...), custom_call_target="tpu_custom_call" | custom-call | flops 1500000000 | bytes 13000000 | tf_op jit(solution)/shard_map/later_columns/pallas_call | solution.py:555
  205.8 5.1 %all-to-all-done.2 = f16[16,240,128]{2,1,0:T(8,128)(2,1)S(1)} async-done(((f16[16,240,128]{2,1,0:T(8,128)(2,1)}), f16[16,240,128]{2,1,0:T(8,128)(2,1)S(1)}, u32[]{:S(2)}, u32[]{:S(2)}) %all-to-all-start.2) | async-done | bytes 983072 | tf_op jit(solution)/shard_map/all_to_all | solution.py:614
  211.2 2.1 %put_in_order.1 = f32[64,7168]{1,0:T(8,128)} custom-call(f32[1]{0:T(128)} %bitcast.19.scale_ref, f32[16,128,128]{2,1,0:T(8,128)S(1)} %convert_multiply_fusion.a_ref, f32[16,96,128]{2,1,0:T(8,128)S(1)} %convert_multiply_fusion.1.b_ref), custom_call_target="tpu_custom_call" | custom-call | tf_op jit(solution)/shard_map/put_in_order/pallas_call | solution.py:434
  (44 shorter events, 3.2 us)
Async XLA Ops:
  0.7 0.7 copy-start.1
  90.4 26.3 %all-to-all-start.1 = ((bf16[16,384,128]{2,1,0:T(8,128)(2,1)}), bf16[16,384,128]{2,1,0:T(8,128)(2,1)S(1)}, u32[]{:S(2)}, u32[]{:S(2)}) async-start(bf16[16,384,128]{2,1,0:T(8,128)(2,1)} %get-tuple-element.81), calls=%async_computation.1 | async-start | bytes 3145728 | tf_op jit(solution)/shard_map/all_to_all | solution.py:585
  94.1 23.1 %copy-start.4 = (f32[1,128,880]{1,2,0:T(8,128)S(1)}, f32[1,128,880]{1,2,0:T(8,128)}, u32[]{:S(2)}) copy-start(f32[1,128,880]{1,2,0:T(8,128)} %param.13) | copy-start | bytes 1351684
  116.7 7.4 %collective-permute-start.1 = (f32[4,2064,128]{2,1,0:T(8,128)}, f32[4,2064,128]{2,1,0:T(8,128)S(1)}, u32[]{:S(2)}, u32[]{:S(2)}) collective-permute-start(f32[4,2064,128]{2,1,0:T(8,128)} %get-tuple-element.90), channel_id=1, source_target_pairs={{0,16},{16,0},{1,17},{17,1},{2,18},{18,2},{3,19},{19,3},{4,20},{20... | collective-permute-start | bytes 12681224 | tf_op jit(solution)/shard_map/ppermute | solution.py:386
  116.7 5.9 %collective-permute-start = (f32[8,128]{1,0:T(8,128)S(1)}, f32[8,128]{1,0:T(8,128)S(1)}, u32[]{:S(2)}, u32[]{:S(2)}) collective-permute-start(f32[8,128]{1,0:T(8,128)S(1)} %get-tuple-element.85), channel_id=1, source_target_pairs={{0,16},{16,0},{1,17},{17,1},{2,18},{18,2},{3,19},{19,3},{4,20},{20... | collective-permute-start | bytes 12296 | tf_op jit(solution)/shard_map/ppermute | solution.py:386
  117.2 13.6 %collective-permute-start.5 = (bf16[880,128]{1,0:T(8,128)(2,1)S(1)}, bf16[880,128]{1,0:T(8,128)(2,1)S(1)}, u32[]{:S(2)}, u32[]{:S(2)}) collective-permute-start(bf16[880,128]{1,0:T(8,128)(2,1)S(1)} %convert_bitcast_fusion), channel_id=1, source_target_pairs={{0,96},{32,0},{64,32},{96,64},{1,97},{33,1},{65,33},{97,65},{2,98}... | collective-permute-start | bytes 675848 | tf_op jit(solution)/shard_map/ppermute | solution.py:513
  118.1 25.9 %collective-permute-start.6 = (bf16[880,128]{1,0:T(8,128)(2,1)S(1)}, bf16[880,128]{1,0:T(8,128)(2,1)S(1)}, u32[]{:S(2)}, u32[]{:S(2)}) collective-permute-start(bf16[880,128]{1,0:T(8,128)(2,1)S(1)} %convert_bitcast_fusion), channel_id=1, source_target_pairs={{0,64},{32,96},{64,0},{96,32},{1,65},{33,97},{65,1},{97,33},{2,66}... | collective-permute-start | bytes 675848 | tf_op jit(solution)/shard_map/ppermute | solution.py:513
  119.2 24.8 %collective-permute-start.7 = (bf16[880,128]{1,0:T(8,128)(2,1)S(1)}, bf16[880,128]{1,0:T(8,128)(2,1)S(1)}, u32[]{:S(2)}, u32[]{:S(2)}) collective-permute-start(bf16[880,128]{1,0:T(8,128)(2,1)S(1)} %convert_bitcast_fusion), channel_id=1, source_target_pairs={{0,32},{32,64},{64,96},{96,0},{1,33},{33,65},{65,97},{97,1},{2,34}... | collective-permute-start | bytes 675848 | tf_op jit(solution)/shard_map/ppermute | solution.py:513
  127.6 27.2 %copy-start.5 = (f32[1,128]{1,0:T(1,128)S(1)}, f32[1,128]{1,0:T(1,128)}, u32[]{:S(2)}) copy-start(f32[1,128]{1,0:T(1,128)} %param.11) | copy-start | bytes 1540
  127.6 16.5 %collective-permute-start.2 = (f16[2064,128]{1,0:T(8,128)(2,1)S(1)}, f16[2064,128]{1,0:T(8,128)(2,1)S(1)}, u32[]{:S(2)}, u32[]{:S(2)}) collective-permute-start(f16[2064,128]{1,0:T(8,128)(2,1)S(1)} %get-tuple-element.99), channel_id=1, source_target_pairs={{0,32},{32,64},{64,96},{96,0},{1,33},{33,65},{65,97},{97,1},{2,34}... | collective-permute-start | bytes 1585160 | tf_op jit(solution)/shard_map/ppermute | solution.py:415
  128.1 16.4 %collective-permute-start.3 = (f16[2064,128]{1,0:T(8,128)(2,1)S(1)}, f16[2064,128]{1,0:T(8,128)(2,1)S(1)}, u32[]{:S(2)}, u32[]{:S(2)}) collective-permute-start(f16[2064,128]{1,0:T(8,128)(2,1)S(1)} %get-tuple-element.100), channel_id=1, source_target_pairs={{0,64},{32,96},{64,0},{96,32},{1,65},{33,97},{65,1},{97,33},{2,66}... | collective-permute-start | bytes 1585160 | tf_op jit(solution)/shard_map/ppermute | solution.py:415
  130.8 23.9 %collective-permute-start.4 = (f16[2064,128]{1,0:T(8,128)(2,1)S(1)}, f16[2064,128]{1,0:T(8,128)(2,1)S(1)}, u32[]{:S(2)}, u32[]{:S(2)}) collective-permute-start(f16[2064,128]{1,0:T(8,128)(2,1)S(1)} %get-tuple-element.101), channel_id=1, source_target_pairs={{0,96},{32,0},{64,32},{96,64},{1,97},{33,1},{65,33},{97,65},{2,98}... | collective-permute-start | bytes 1585160 | tf_op jit(solution)/shard_map/ppermute | solution.py:415
  154.7 5.9 %collective-permute-start.8 = (f32[4,1552,128]{2,1,0:T(8,128)}, f32[4,1552,128]{2,1,0:T(8,128)S(1)}, u32[]{:S(2)}, u32[]{:S(2)}) collective-permute-start(f32[4,1552,128]{2,1,0:T(8,128)} %get-tuple-element.105), channel_id=1, source_target_pairs={{0,16},{16,0},{1,17},{17,1},{2,18},{18,2},{3,19},{19,3},{4,20},{20... | collective-permute-start | bytes 9535496 | tf_op jit(solution)/shard_map/ppermute | solution.py:386
  154.8 5.9 %copy-start.3 = (f32[4,1552,128]{2,1,0:T(8,128)S(1)}, f32[4,1552,128]{2,1,0:T(8,128)}, u32[]{:S(2)}) copy-start(f32[4,1552,128]{2,1,0:T(8,128)} %get-tuple-element.104) | copy-start | bytes 9535492
  154.8 5.3 %collective-permute-start.9 = (f32[8,128]{1,0:T(8,128)S(1)}, f32[8,128]{1,0:T(8,128)S(1)}, u32[]{:S(2)}, u32[]{:S(2)}) collective-permute-start(f32[8,128]{1,0:T(8,128)S(1)} %get-tuple-element.106), channel_id=1, source_target_pairs={{0,16},{16,0},{1,17},{17,1},{2,18},{18,2},{3,19},{19,3},{4,20},{20... | collective-permute-start | bytes 12296 | tf_op jit(solution)/shard_map/ppermute | solution.py:386
  161.9 3.6 %copy-start = (f32[1,128,128]{2,1,0:T(8,128)S(1)}, f32[1,128,128]{2,1,0:T(8,128)}, u32[]{:S(2)}) copy-start(f32[1,128,128]{2,1,0:T(8,128)} %param.12) | copy-start | bytes 196612
  161.9 3.6 %copy-start.2 = (s32[1,256]{1,0:T(1,128)S(1)}, s32[1,256]{1,0:T(1,128)}, u32[]{:S(2)}) copy-start(s32[1,256]{1,0:T(1,128)} %levels_ref) | copy-start | bytes 3076
  162.1 23.5 %collective-permute-start.13 = (bf16[4,880,128]{2,1,0:T(8,128)(2,1)S(1)}, bf16[4,880,128]{2,1,0:T(8,128)(2,1)S(1)}, u32[]{:S(2)}, u32[]{:S(2)}) collective-permute-start(bf16[4,880,128]{2,1,0:T(8,128)(2,1)S(1)} %pad_maximum_fusion.1.own_ref), channel_id=1, source_target_pairs={{0,16},{16,0},{1,17},{17,1},{2,18},{18,2},{3,19},{19,3},{4,20},{20... | collective-permute-start | bytes 2703368 | tf_op jit(solution)/shard_map/ppermute | solution.py:606
  162.3 19.6 %collective-permute-start.10 = (f16[1552,128]{1,0:T(8,128)(2,1)S(1)}, f16[1552,128]{1,0:T(8,128)(2,1)S(1)}, u32[]{:S(2)}, u32[]{:S(2)}) collective-permute-start(f16[1552,128]{1,0:T(8,128)(2,1)S(1)} %get-tuple-element.121), channel_id=1, source_target_pairs={{0,32},{32,64},{64,96},{96,0},{1,33},{33,65},{65,97},{97,1},{2,34}... | collective-permute-start | bytes 1191944 | tf_op jit(solution)/shard_map/ppermute | solution.py:415
  164.3 17.5 %collective-permute-start.11 = (f16[1552,128]{1,0:T(8,128)(2,1)S(1)}, f16[1552,128]{1,0:T(8,128)(2,1)S(1)}, u32[]{:S(2)}, u32[]{:S(2)}) collective-permute-start(f16[1552,128]{1,0:T(8,128)(2,1)S(1)} %get-tuple-element.122), channel_id=1, source_target_pairs={{0,64},{32,96},{64,0},{96,32},{1,65},{33,97},{65,1},{97,33},{2,66}... | collective-permute-start | bytes 1191944 | tf_op jit(solution)/shard_map/ppermute | solution.py:415
  165.3 20.2 %collective-permute-start.12 = (f16[1552,128]{1,0:T(8,128)(2,1)S(1)}, f16[1552,128]{1,0:T(8,128)(2,1)S(1)}, u32[]{:S(2)}, u32[]{:S(2)}) collective-permute-start(f16[1552,128]{1,0:T(8,128)(2,1)S(1)} %get-tuple-element.123), channel_id=1, source_target_pairs={{0,96},{32,0},{64,32},{96,64},{1,97},{33,1},{65,33},{97,65},{2,98}... | collective-permute-start | bytes 1191944 | tf_op jit(solution)/shard_map/ppermute | solution.py:415
  187.2 23.7 %all-to-all-start.2 = ((f16[16,240,128]{2,1,0:T(8,128)(2,1)}), f16[16,240,128]{2,1,0:T(8,128)(2,1)S(1)}, u32[]{:S(2)}, u32[]{:S(2)}) async-start(f16[16,240,128]{2,1,0:T(8,128)(2,1)} %pad_maximum_fusion), calls=%async_computation.2 | async-start | bytes 1966080 | tf_op jit(solution)/shard_map/all_to_all | solution.py:614
